TPU v7x, 512 devices: a whole 4x4x16 slice. The times are simulated.
512 devices in a mesh: tm: 8 (over x, core), dom: 64 (over y, z).
Axes of the slice: x: 4, y: 4, z: 16, core: 2. Of those that a mesh axis runs over, the one named last changes fastest.
Arguments:
- memory_start: bfloat16 [131072, 256], P('dom'), may hold values from -40 to 40
- src_row: int32 [8, 16384], P('tm', 'dom'), may hold values from 0 to 2047
- dst_pos: int32 [8, 16384], P('tm', 'dom'), may hold values from 0 to 8191, as said below
- neg_pos: int32 [8, 16384], P('tm', 'dom'), may hold values from 0 to 8191, as said below
- nbr_pos: int32 [8, 16384, 32], P('tm', 'dom'), may hold values from 0 to 8191, as said below
- event_time: int32 [8, 16384], P('tm', 'dom'), may hold values from 4096 to 8191
- nbr_time: int32 [8, 16384, 32], P('tm', 'dom'), may hold values from 0 to 4095
- edge_feat: bfloat16 [8, 16384, 172], P('tm', 'dom'), may hold values from -6 to 6
- tile_req: int32 [8, 64, 64], P('tm', 'dom'), may hold values from 0 to 15
- tile_count: int32 [8, 64, 64], P('tm', 'dom'), may hold values from 0 to 1, as said below
- time_freq: float32 [128], replicated, may hold values from 0.0001 to 0.3
- time_phase: float32 [128], replicated, may hold values from -3.140625 to 3.140625
- msg_memory: bfloat16 [512, 768], replicated, may hold values from -0.21875 to 0.21875
- msg_time: bfloat16 [128, 768], replicated, may hold values from -0.21875 to 0.21875
- msg_edge: bfloat16 [172, 768], replicated, may hold values from -0.21875 to 0.21875
- bias_input: float32 [768], replicated, may hold values from -3 to 3
- hid_weight: bfloat16 [256, 768], replicated, may hold values from -0.375 to 0.375
- bias_hidden: float32 [768], replicated, may hold values from -3 to 3
- query_weight: bfloat16 [256, 256], replicated, may hold values from -0.375 to 0.375
- keyval_weight: bfloat16 [384, 512], replicated, may hold values from -0.3125 to 0.3125
- out_weight: bfloat16 [512, 256], replicated, may hold values from -0.25 to 0.25
- bias_out: float32 [256], replicated, may hold values from -3 to 3
- pred_weight: bfloat16 [512, 256], replicated, may hold values from -0.25 to 0.25
- bias_pred: float32 [256], replicated, may hold values from -3 to 3
- logit_weight: bfloat16 [256], replicated, may hold values from -0.375 to 0.375
Outputs:
- logits: float32 [2, 8, 16384], P(None, 'tm', 'dom')
- memory_after: bfloat16 [8, 131072, 256], P('tm', 'dom')
Inputs may be any that keep to these rules, and one draw needn't show every extreme that they name: `tile_count`: 0 or 1; in each batch one owner has count 1 from every device, and one device has count 1 for every owner. `dst_pos`: below 128 times the number of owners with tile count 1 for the event's device and batch; that bound minus one is taken by some event of every device in every batch. `neg_pos`: below 128 times the number of owners with tile count 1 for the event's device and batch; that bound minus one is taken by some event of every device in every batch. `nbr_pos`: below 128 times the number of owners with tile count 1 for the event's device and batch; that bound minus one is taken by some neighbour on every device in every batch.
All inputs are finite; a program needn't handle non-finite values.
Results may differ from a plain program's by a relative error of at most 0.0075.
Values may be sent and summed in bfloat16 or wider, within the bound.
No kernel may reach another device: no remote copies, remote signals or barrier semaphores. Data moves between devices by JAX's collectives and lax.ppermute only.
A program may use at most 192 MiB of HBM per device.

v0:
```python
import jax
import jax.numpy as jnp
from jax import lax
from jax.sharding import PartitionSpec as P

HEADS = 2
TILE = 128


def passed_along(value, axis, steps):
    count = lax.axis_size(axis)
    first, last = (max(0, -steps), min(count, count - steps))
    return lax.ppermute(value, axis, [(source, source + steps) for source in range(first, last)])


def time_code(delta, time_freq, time_phase):
    angle = delta.astype(jnp.float32)[..., None] * time_freq + time_phase
    return jnp.cos(angle).astype(jnp.bfloat16)


def padded_rows(position, counts, tile_rows):
    running = jnp.cumsum(counts)
    tile_index = position // tile_rows
    owner_id = jnp.sum((running <= tile_index[..., None]).astype(jnp.int32), axis=-1)
    return owner_id * tile_rows + position % tile_rows


def gru_update(gate_in, gate_hid, state):
    state_width = state.shape[1]
    reset_gate = jax.nn.sigmoid(gate_in[:, :state_width] + gate_hid[:, :state_width])
    keep_gate = jax.nn.sigmoid(
        gate_in[:, state_width : 2 * state_width] + gate_hid[:, state_width : 2 * state_width]
    )
    candidate = jnp.tanh(
        gate_in[:, 2 * state_width :] + reset_gate * gate_hid[:, 2 * state_width :]
    )
    return (1.0 - keep_gate) * candidate + keep_gate * state.astype(jnp.float32)


def later_wins(earlier, later):
    return (
        jnp.where(later[1][:, None] > 0, later[0], earlier[0]),
        jnp.maximum(earlier[1], later[1]),
    )


def shards(
    memory_start,
    src_row,
    dst_pos,
    neg_pos,
    nbr_pos,
    event_time,
    nbr_time,
    edge_feat,
    tile_req,
    tile_count,
    time_freq,
    time_phase,
    msg_memory,
    msg_time,
    msg_edge,
    bias_input,
    hid_weight,
    bias_hidden,
    query_weight,
    keyval_weight,
    out_weight,
    bias_out,
    pred_weight,
    bias_pred,
    logit_weight,
):
    owners = lax.axis_size("dom")
    node_rows, mem_width = memory_start.shape
    events = src_row.shape[1]
    neighbours = nbr_pos.shape[2]
    tile_rows = TILE
    head_width = mem_width // HEADS
    wanted = tile_req.reshape(owners)
    counts = tile_count.reshape(owners)
    asked_tiles = lax.all_to_all(
        wanted.reshape(owners, 1), "dom", split_axis=0, concat_axis=0, tiled=True
    ).reshape(owners)
    tile_block = memory_start.reshape(node_rows // tile_rows, tile_rows, mem_width)[asked_tiles]
    fetched = lax.all_to_all(tile_block, "dom", split_axis=0, concat_axis=0, tiled=True)
    fetched_rows = fetched.reshape(owners * tile_rows, mem_width)
    sources = src_row.reshape(events)
    event_times = event_time.reshape(events)
    past_times = nbr_time.reshape(events, neighbours)
    dst_rows = padded_rows(dst_pos.reshape(events), counts, tile_rows)
    neg_rows = padded_rows(neg_pos.reshape(events), counts, tile_rows)
    nbr_rows = padded_rows(nbr_pos.reshape(events, neighbours), counts, tile_rows)
    source_mem = memory_start[sources]
    target_mem = fetched_rows[dst_rows]
    message_code = time_code(event_times - past_times[:, 0], time_freq, time_phase)
    pre_gate = jnp.dot(source_mem, msg_memory[:mem_width], preferred_element_type=jnp.float32)
    pre_gate = pre_gate + jnp.dot(
        target_mem, msg_memory[mem_width:], preferred_element_type=jnp.float32
    )
    pre_gate = pre_gate + jnp.dot(message_code, msg_time, preferred_element_type=jnp.float32)
    pre_gate = pre_gate + jnp.dot(
        edge_feat.reshape(events, -1), msg_edge, preferred_element_type=jnp.float32
    )
    pre_gate = pre_gate + bias_input
    summed = jax.ops.segment_sum(pre_gate, sources, num_segments=node_rows)
    tallies = jax.ops.segment_sum(jnp.ones((events,), jnp.float32), sources, num_segments=node_rows)
    gate_in = summed / jnp.maximum(tallies, 1.0)[:, None]
    gate_hid = jnp.dot(memory_start, hid_weight, preferred_element_type=jnp.float32) + bias_hidden
    written = gru_update(gate_in, gate_hid, memory_start).astype(jnp.bfloat16)
    touched = (tallies > 0.0).astype(jnp.bfloat16)
    zero_rows = jnp.zeros_like(written)
    zero_flags = jnp.zeros_like(touched)
    carried_mem, carried_flag = (zero_rows, zero_flags)
    for hop_index in range(lax.axis_size("tm") - 1):
        joined_mem, joined_flag = later_wins((carried_mem, carried_flag), (written, touched))
        carried_mem, carried_flag = passed_along((joined_mem, joined_flag), "tm", 1)
    before = jnp.where(carried_flag[:, None] > 0, carried_mem, memory_start)
    memory_after = jnp.where(touched[:, None] > 0, written, before)
    current_src = before[sources]
    queries = jnp.dot(current_src, query_weight, preferred_element_type=jnp.float32).astype(
        jnp.bfloat16
    )
    block_size = min(64, events)
    block_count = events // block_size
    age_values = event_times[:, None] - past_times

    def attend(packed):
        rows_block, ages_block, query_block = packed
        neighbour_mem = fetched_rows[rows_block.reshape(-1)]
        neighbour_code = time_code(ages_block.reshape(-1), time_freq, time_phase)
        keyval = jnp.dot(
            neighbour_mem, keyval_weight[:mem_width], preferred_element_type=jnp.float32
        )
        keyval = keyval + jnp.dot(
            neighbour_code, keyval_weight[mem_width:], preferred_element_type=jnp.float32
        )
        keyval = keyval.astype(jnp.bfloat16).reshape(block_size, neighbours, 2, HEADS, head_width)
        key_heads = keyval[:, :, 0]
        value_heads = keyval[:, :, 1]
        query_heads = query_block.reshape(block_size, HEADS, head_width)
        scores = jnp.einsum(
            "ehc,enhc->ehn", query_heads, key_heads, preferred_element_type=jnp.float32
        )
        scores = scores / jnp.sqrt(jnp.float32(head_width))
        row_max = jnp.max(scores, axis=-1, keepdims=True)
        exponent = jnp.exp(scores - row_max)
        weights = (exponent / jnp.sum(exponent, axis=-1, keepdims=True)).astype(jnp.bfloat16)
        mixed = jnp.einsum(
            "ehn,enhc->ehc", weights, value_heads, preferred_element_type=jnp.float32
        )
        return mixed.reshape(block_size, mem_width).astype(jnp.bfloat16)

    attended = lax.map(
        attend,
        (
            nbr_rows.reshape(block_count, block_size, neighbours),
            age_values.reshape(block_count, block_size, neighbours),
            queries.reshape(block_count, block_size, mem_width),
        ),
    )
    attended = attended.reshape(events, mem_width)
    embedding = jnp.dot(attended, out_weight[:mem_width], preferred_element_type=jnp.float32)
    embedding = embedding + jnp.dot(
        current_src, out_weight[mem_width:], preferred_element_type=jnp.float32
    )
    embedding = jax.nn.relu(embedding + bias_out).astype(jnp.bfloat16)
    embed_part = jnp.dot(embedding, pred_weight[:mem_width], preferred_element_type=jnp.float32)

    def predict(other_mem):
        hidden_pred = embed_part + jnp.dot(
            other_mem, pred_weight[mem_width:], preferred_element_type=jnp.float32
        )
        hidden_pred = jax.nn.relu(hidden_pred + bias_pred).astype(jnp.bfloat16)
        return jnp.dot(hidden_pred, logit_weight, preferred_element_type=jnp.float32)

    logits = jnp.stack([predict(target_mem), predict(fetched_rows[neg_rows])]).reshape(2, 1, events)
    return (logits, memory_after.reshape(1, node_rows, mem_width))


def solution(mesh):
    in_specs = (
        P("dom", None),
        P("tm", "dom"),
        P("tm", "dom"),
        P("tm", "dom"),
        P("tm", "dom", None),
        P("tm", "dom"),
        P("tm", "dom", None),
        P("tm", "dom", None),
        P("tm", "dom", None),
        P("tm", "dom", None),
        P(),
        P(),
        P(),
        P(),
        P(),
        P(),
        P(),
        P(),
        P(),
        P(),
        P(),
        P(),
        P(),
        P(),
        P(),
    )
    out_specs = (P(None, "tm", "dom"), P("tm", "dom", None))
    return jax.shard_map(shards, mesh=mesh, in_specs=in_specs, out_specs=out_specs, check_vma=False)
```

profile of v0, /device:TPU:1, one launch (start us, length us, event | category | flops | bytes accessed | tf_op | source)
XLA Modules:
  0.0 521.8 jit_solution(2882609332806902139)
XLA Ops:
  2.1 19.3 %all-to-all-start = ((s32[64,1,1]{2,1,0:T(1,128)}), s32[64,1,1]{2,1,0:T(1,128)S(1)}, u32[]{:S(2)}, u32[]{:S(2)}) async-start(s32[64,1,1]{2,1,0:T(1,128)} %copy.45), calls=%async_computation | async-start | bytes 65536 | tf_op jit(solution)/shard_map/all_to_all | solution.py:82
  21.3 13.2 %all-to-all-done = s32[64,1,1]{2,1,0:T(1,128)S(1)} async-done(((s32[64,1,1]{2,1,0:T(1,128)}), s32[64,1,1]{2,1,0:T(1,128)S(1)}, u32[]{:S(2)}, u32[]{:S(2)}) %all-to-all-start) | async-done | bytes 288 | tf_op jit(solution)/shard_map/all_to_all | solution.py:82
  35.8 4.1 gather_fusion.2
  39.9 5.8 %all-to-all-start.1 = ((bf16[64,128,256]{2,1,0:T(8,128)(2,1)}), bf16[64,128,256]{2,1,0:T(8,128)(2,1)}, u32[]{:S(2)}, u32[]{:S(2)}) async-start(bf16[64,128,256]{2,1,0:T(8,128)(2,1)} %gather_fusion.2), calls=%async_computation.1 | async-start | bytes 8388608 | tf_op jit(solution)/shard_map/all_to_all | solution.py:86
  47.3 1.9 scatter_custom_fusion
  51.1 3.6 convolution_add_fusion
  54.7 172.6 %all-to-all-done.1 = bf16[64,128,256]{2,1,0:T(8,128)(2,1)} async-done(((bf16[64,128,256]{2,1,0:T(8,128)(2,1)}), bf16[64,128,256]{2,1,0:T(8,128)(2,1)}, u32[]{:S(2)}, u32[]{:S(2)}) %all-to-all-start.1) | async-done | bytes 4194336 | tf_op jit(solution)/shard_map/all_to_all | solution.py:86
  227.3 3.7 gather_fusion.3
  232.4 5.2 scatter_custom_fusion.1
  237.6 3.3 broadcast_divide_fusion
  240.9 3.7 broadcast_select_fusion.6
  244.6 10.2 %collective-permute-start.7 = (bf16[2048,256]{1,0:T(8,128)(2,1)S(1)}, bf16[2048,256]{1,0:T(8,128)(2,1)S(1)}, u32[]{:S(2)}, u32[]{:S(2)}) collective-permute-start(bf16[2048,256]{1,0:T(8,128)(2,1)S(1)} %get-tuple-element.74), channel_id=1, source_target_pairs={{0,64},{64,128},{128,192},{192,256},{256,320},{320,384},{384,448},... | collective-permute-start | bytes 3145736 | tf_op jit(solution)/shard_map/ppermute | solution.py:13
  254.8 11.7 %collective-permute-done.7 = bf16[2048,256]{1,0:T(8,128)(2,1)S(1)} collective-permute-done((bf16[2048,256]{1,0:T(8,128)(2,1)S(1)}, bf16[2048,256]{1,0:T(8,128)(2,1)S(1)}, u32[]{:S(2)}, u32[]{:S(2)}) %collective-permute-start.7) | collective-permute-done | bytes 1048608 | tf_op jit(solution)/shard_map/ppermute | solution.py:13
  267.0 4.4 collective-permute-start.8
  271.4 11.7 %collective-permute-done.8 = bf16[2048,256]{1,0:T(8,128)(2,1)S(1)} collective-permute-done((bf16[2048,256]{1,0:T(8,128)(2,1)S(1)}, bf16[2048,256]{1,0:T(8,128)(2,1)S(1)}, u32[]{:S(2)}, u32[]{:S(2)}) %collective-permute-start.8) | collective-permute-done | bytes 1048608 | tf_op jit(solution)/shard_map/ppermute | solution.py:13
  283.5 4.4 collective-permute-start.9
  287.9 11.7 %collective-permute-done.9 = bf16[2048,256]{1,0:T(8,128)(2,1)S(1)} collective-permute-done((bf16[2048,256]{1,0:T(8,128)(2,1)S(1)}, bf16[2048,256]{1,0:T(8,128)(2,1)S(1)}, u32[]{:S(2)}, u32[]{:S(2)}) %collective-permute-start.9) | collective-permute-done | bytes 1048608 | tf_op jit(solution)/shard_map/ppermute | solution.py:13
  300.1 4.4 collective-permute-start.10
  304.5 11.7 %collective-permute-done.10 = bf16[2048,256]{1,0:T(8,128)(2,1)S(1)} collective-permute-done((bf16[2048,256]{1,0:T(8,128)(2,1)S(1)}, bf16[2048,256]{1,0:T(8,128)(2,1)S(1)}, u32[]{:S(2)}, u32[]{:S(2)}) %collective-permute-start.10) | collective-permute-done | bytes 1048608 | tf_op jit(solution)/shard_map/ppermute | solution.py:13
  316.6 4.4 collective-permute-start.11
  321.0 1.9 collective-permute-start
  323.0 9.8 %collective-permute-done = bf16[2048]{0:T(1024)(128)(2,1)S(1)} collective-permute-done((bf16[2048]{0:T(1024)(128)(2,1)S(1)}, bf16[2048]{0:T(1024)(128)(2,1)S(1)}, u32[]{:S(2)}, u32[]{:S(2)}) %collective-permute-start) | collective-permute-done | bytes 4128 | tf_op jit(solution)/shard_map/ppermute | solution.py:13
  332.8 4.4 collective-permute-start.1
  337.7 1.9 collective-permute-start.12
  339.7 3.5 collective-permute-start.2
  343.5 7.8 %collective-permute-done.2 = bf16[2048]{0:T(1024)(128)(2,1)S(1)} collective-permute-done((bf16[2048]{0:T(1024)(128)(2,1)S(1)}, bf16[2048]{0:T(1024)(128)(2,1)S(1)}, u32[]{:S(2)}, u32[]{:S(2)}) %collective-permute-start.2) | collective-permute-done | bytes 4128 | tf_op jit(solution)/shard_map/ppermute | solution.py:13
  352.0 4.4 collective-permute-start.3
  357.0 1.5 copy.47
  358.5 1.5 copy.49
  362.0 1.9 reduce.5
  366.0 1.9 collective-permute-start.4
  368.0 2.3 broadcast_select_fusion
  370.2 3.5 collective-permute-start.13
  373.9 1.9 collective-permute-start.5
  376.5 9.2 %collective-permute-done.5 = bf16[2048]{0:T(1024)(128)(2,1)S(1)} collective-permute-done((bf16[2048]{0:T(1024)(128)(2,1)S(1)}, bf16[2048]{0:T(1024)(128)(2,1)S(1)}, u32[]{:S(2)}, u32[]{:S(2)}) %collective-permute-start.5) | collective-permute-done | bytes 4128 | tf_op jit(solution)/shard_map/ppermute | solution.py:13
  385.8 4.4 collective-permute-start.6
  391.4 4.3 gather_fusion.5
  395.8 4.1 select_bitcast_fusion
  399.9 2.5 gather_fusion.4
  403.2 112.8 %while.10 = (s32[]{:T(128)}, bf16[4,64,256]{2,1,0:T(8,128)(2,1)}, bf16[4,64,256]{2,1,0:T(8,128)(2,1)}, s32[4,64,32]{2,1,0:T(8,128)S(1)}, bf16[8192,256]{1,0:T(8,...) while((s32[]{:T(128)}, bf16[4,64,256]{2,1,0:T(8,128)(2,1)}, ...), condition=%wide.region_8.9_spmd, body=%wide.region_5.8_spmd.sunk | while | flops 810330432 | bytes 27281152 | solution.py:154
  403.4 9.4 %gather_fusion = bf16[2048,256]{1,0:T(8,128)(2,1)S(1)} fusion(bf16[8192,256]{1,0:T(8,128)(2,1)} %get-tuple-element.171, s32[2048]{0:T(1024)S(1)} %broadcast_clamp_fusion.2), kind=kCustom, calls=%fused_computation.clone.1 | custom fusion | bytes 2105344 | tf_op jit(solution)/shard_map/while/body/eval_jaxpr/gather | solution.py:130
  412.8 2.7 fusion.122
  415.5 6.7 %add_convert_fusion.2 = bf16[2048,512]{1,0:T(8,128)(2,1)} fusion(f32[2048,512]{1,0:T(8,128)} %fusion.122, f32[128]{0:T(128)S(1)} %get-tuple-element.175, f32[128]{0:T(128)S(1)} %get-tuple-element.174, f32[2048]{0:T(1024)S(1)} %convert_element_type.127, bf16[384,512]{1,0:T(8,128)(2,1)S(1)} %get-tuple-element.172), kind=kOutput, calls=%fused_computation.10.clone.1 | convolution fusion | flops 271319040 | bytes 6431744 | tf_op jit(solution)/shard_map/while/body/eval_jaxpr/dot_general | solution.py:135
  422.2 2.5 reshape.571
  424.7 2.7 slice_bitcast_fusion.3
  428.2 1.9 fusion.123
  431.6 9.4 %gather_fusion = bf16[2048,256]{1,0:T(8,128)(2,1)S(1)} fusion(bf16[8192,256]{1,0:T(8,128)(2,1)} %get-tuple-element.171, s32[2048]{0:T(1024)S(1)} %broadcast_clamp_fusion.2), kind=kCustom, calls=%fused_computation.clone.1 | custom fusion | bytes 2105344 | tf_op jit(solution)/shard_map/while/body/eval_jaxpr/gather | solution.py:130
  441.0 2.6 fusion.122
  443.7 6.7 %add_convert_fusion.2 = bf16[2048,512]{1,0:T(8,128)(2,1)} fusion(f32[2048,512]{1,0:T(8,128)} %fusion.122, f32[128]{0:T(128)S(1)} %get-tuple-element.175, f32[128]{0:T(128)S(1)} %get-tuple-element.174, f32[2048]{0:T(1024)S(1)} %convert_element_type.127, bf16[384,512]{1,0:T(8,128)(2,1)S(1)} %get-tuple-element.172), kind=kOutput, calls=%fused_computation.10.clone.1 | convolution fusion | flops 271319040 | bytes 6431744 | tf_op jit(solution)/shard_map/while/body/eval_jaxpr/dot_general | solution.py:135
  450.4 2.5 reshape.571
  452.9 2.7 slice_bitcast_fusion.3
  456.4 1.9 fusion.123
  459.8 9.4 %gather_fusion = bf16[2048,256]{1,0:T(8,128)(2,1)S(1)} fusion(bf16[8192,256]{1,0:T(8,128)(2,1)} %get-tuple-element.171, s32[2048]{0:T(1024)S(1)} %broadcast_clamp_fusion.2), kind=kCustom, calls=%fused_computation.clone.1 | custom fusion | bytes 2105344 | tf_op jit(solution)/shard_map/while/body/eval_jaxpr/gather | solution.py:130
  469.2 2.6 fusion.122
  471.9 6.7 %add_convert_fusion.2 = bf16[2048,512]{1,0:T(8,128)(2,1)} fusion(f32[2048,512]{1,0:T(8,128)} %fusion.122, f32[128]{0:T(128)S(1)} %get-tuple-element.175, f32[128]{0:T(128)S(1)} %get-tuple-element.174, f32[2048]{0:T(1024)S(1)} %convert_element_type.127, bf16[384,512]{1,0:T(8,128)(2,1)S(1)} %get-tuple-element.172), kind=kOutput, calls=%fused_computation.10.clone.1 | convolution fusion | flops 271319040 | bytes 6431744 | tf_op jit(solution)/shard_map/while/body/eval_jaxpr/dot_general | solution.py:135
  478.6 2.5 reshape.571
  481.1 2.7 slice_bitcast_fusion.3
  484.6 1.9 fusion.123
  488.0 9.4 %gather_fusion = bf16[2048,256]{1,0:T(8,128)(2,1)S(1)} fusion(bf16[8192,256]{1,0:T(8,128)(2,1)} %get-tuple-element.171, s32[2048]{0:T(1024)S(1)} %broadcast_clamp_fusion.2), kind=kCustom, calls=%fused_computation.clone.1 | custom fusion | bytes 2105344 | tf_op jit(solution)/shard_map/while/body/eval_jaxpr/gather | solution.py:130
  497.4 2.6 fusion.122
  500.1 6.7 %add_convert_fusion.2 = bf16[2048,512]{1,0:T(8,128)(2,1)} fusion(f32[2048,512]{1,0:T(8,128)} %fusion.122, f32[128]{0:T(128)S(1)} %get-tuple-element.175, f32[128]{0:T(128)S(1)} %get-tuple-element.174, f32[2048]{0:T(1024)S(1)} %convert_element_type.127, bf16[384,512]{1,0:T(8,128)(2,1)S(1)} %get-tuple-element.172), kind=kOutput, calls=%fused_computation.10.clone.1 | convolution fusion | flops 271319040 | bytes 6431744 | tf_op jit(solution)/shard_map/while/body/eval_jaxpr/dot_general | solution.py:135
  506.8 2.5 reshape.571
  509.3 2.7 slice_bitcast_fusion.3
  512.8 1.9 fusion.123
  (216 shorter events, 33.1 us)
Async XLA Ops:
  0.6 50.5 %copy-start = (bf16[256,768]{1,0:T(8,128)(2,1)S(1)}, bf16[256,768]{1,0:T(8,128)(2,1)}, u32[]{:S(2)}) copy-start(bf16[256,768]{1,0:T(8,128)(2,1)} %param.43) | copy-start | bytes 1179652
  2.1 32.5 %all-to-all-start = ((s32[64,1,1]{2,1,0:T(1,128)}), s32[64,1,1]{2,1,0:T(1,128)S(1)}, u32[]{:S(2)}, u32[]{:S(2)}) async-start(s32[64,1,1]{2,1,0:T(1,128)} %copy.45), calls=%async_computation | async-start | bytes 65536 | tf_op jit(solution)/shard_map/all_to_all | solution.py:82
  39.9 5.9 %copy-start.33 = (s32[1,1,64]{2,1,0:T(1,128)S(1)}, s32[1,1,64]{2,1,0:T(1,128)}, u32[]{:S(2)}) copy-start(s32[1,1,64]{2,1,0:T(1,128)} %param.36) | copy-start | bytes 772
  39.9 6.2 %copy-start.32 = (s32[1,256]{1,0:T(1,128)S(1)}, s32[1,256]{1,0:T(1,128)}, u32[]{:S(2)}) copy-start(s32[1,256]{1,0:T(1,128)} %param.28) | copy-start | bytes 3076
  39.9 6.2 %copy-start.1 = (bf16[2048,256]{1,0:T(8,128)(2,1)S(1)}, bf16[2048,256]{1,0:T(8,128)(2,1)}, u32[]{:S(2)}) copy-start(bf16[2048,256]{1,0:T(8,128)(2,1)} %param.27) | copy-start | bytes 3145732
  39.9 9.4 %copy-start.31 = (s32[1,256]{1,0:T(1,128)S(1)}, s32[1,256]{1,0:T(1,128)}, u32[]{:S(2)}) copy-start(s32[1,256]{1,0:T(1,128)} %param.30) | copy-start | bytes 3076
  39.9 9.4 %copy-start.29 = (s32[1,256]{1,0:T(1,128)S(1)}, s32[1,256]{1,0:T(1,128)}, u32[]{:S(2)}) copy-start(s32[1,256]{1,0:T(1,128)} %param.29) | copy-start | bytes 3076
  39.9 10.2 %copy-start.30 = (s32[1,256]{1,0:T(1,128)S(1)}, s32[1,256]{1,0:T(1,128)}, u32[]{:S(2)}) copy-start(s32[1,256]{1,0:T(1,128)} %param.32) | copy-start | bytes 3076
  39.9 10.9 %copy-start.6 = (bf16[512,768]{1,0:T(8,128)(2,1)S(1)}, bf16[512,768]{1,0:T(8,128)(2,1)}, u32[]{:S(2)}) copy-start(bf16[512,768]{1,0:T(8,128)(2,1)} %param.39) | copy-start | bytes 2359300
  39.9 187.4 %all-to-all-start.1 = ((bf16[64,128,256]{2,1,0:T(8,128)(2,1)}), bf16[64,128,256]{2,1,0:T(8,128)(2,1)}, u32[]{:S(2)}, u32[]{:S(2)}) async-start(bf16[64,128,256]{2,1,0:T(8,128)(2,1)} %gather_fusion.2), calls=%async_computation.1 | async-start | bytes 8388608 | tf_op jit(solution)/shard_map/all_to_all | solution.py:86
  45.8 5.3 %copy-start.21 = (f32[768]{0:T(1024)S(1)}, f32[768]{0:T(1024)}, u32[]{:S(2)}) copy-start(f32[768]{0:T(1024)} %param.44) | copy-start | bytes 9220
  46.1 5.0 copy-start.24
  46.2 1.2 copy-start.22
  54.7 176.6 %copy-start.15 = (bf16[128,768]{1,0:T(8,128)(2,1)S(1)}, bf16[128,768]{1,0:T(8,128)(2,1)}, u32[]{:S(2)}) copy-start(bf16[128,768]{1,0:T(8,128)(2,1)} %param.40) | copy-start | bytes 589828
  54.7 176.6 %copy-start.19 = (f32[128]{0:T(128)S(1)}, f32[128]{0:T(128)}, u32[]{:S(2)}) copy-start(f32[128]{0:T(128)} %param.38) | copy-start | bytes 1540
  54.7 176.6 %copy-start.20 = (f32[128]{0:T(128)S(1)}, f32[128]{0:T(128)}, u32[]{:S(2)}) copy-start(f32[128]{0:T(128)} %param.37) | copy-start | bytes 1540
  231.0 1.4 copy-start.4
  231.0 1.0 copy-start.14
  231.0 1.0 copy-start.18
  231.0 1.0 copy-start.26
  244.6 22.0 %collective-permute-start.7 = (bf16[2048,256]{1,0:T(8,128)(2,1)S(1)}, bf16[2048,256]{1,0:T(8,128)(2,1)S(1)}, u32[]{:S(2)}, u32[]{:S(2)}) collective-permute-start(bf16[2048,256]{1,0:T(8,128)(2,1)S(1)} %get-tuple-element.74), channel_id=1, source_target_pairs={{0,64},{64,128},{128,192},{192,256},{256,320},{320,384},{384,448},... | collective-permute-start | bytes 3145736 | tf_op jit(solution)/shard_map/ppermute | solution.py:13
  267.0 16.1 %collective-permute-start.8 = (bf16[2048,256]{1,0:T(8,128)(2,1)S(1)}, bf16[2048,256]{1,0:T(8,128)(2,1)S(1)}, u32[]{:S(2)}, u32[]{:S(2)}) collective-permute-start(bf16[2048,256]{1,0:T(8,128)(2,1)S(1)} %broadcast_select_fusion.5), channel_id=1, source_target_pairs={{0,64},{64,128},{128,192},{192,256},{256,320},{320,384},{384,448},... | collective-permute-start | bytes 3145736 | tf_op jit(solution)/shard_map/ppermute | solution.py:13
  283.5 16.1 %collective-permute-start.9 = (bf16[2048,256]{1,0:T(8,128)(2,1)S(1)}, bf16[2048,256]{1,0:T(8,128)(2,1)S(1)}, u32[]{:S(2)}, u32[]{:S(2)}) collective-permute-start(bf16[2048,256]{1,0:T(8,128)(2,1)S(1)} %broadcast_select_fusion.4), channel_id=1, source_target_pairs={{0,64},{64,128},{128,192},{192,256},{256,320},{320,384},{384,448},... | collective-permute-start | bytes 3145736 | tf_op jit(solution)/shard_map/ppermute | solution.py:13
  300.1 16.1 %collective-permute-start.10 = (bf16[2048,256]{1,0:T(8,128)(2,1)S(1)}, bf16[2048,256]{1,0:T(8,128)(2,1)S(1)}, u32[]{:S(2)}, u32[]{:S(2)}) collective-permute-start(bf16[2048,256]{1,0:T(8,128)(2,1)S(1)} %broadcast_select_fusion.3), channel_id=1, source_target_pairs={{0,64},{64,128},{128,192},{192,256},{256,320},{320,384},{384,448},... | collective-permute-start | bytes 3145736 | tf_op jit(solution)/shard_map/ppermute | solution.py:13
  316.6 23.0 %copy-start.17 = (s32[1,256,32]{1,2,0:T(8,128)S(1)}, s32[1,256,32]{1,2,0:T(8,128)}, u32[]{:S(2)}) copy-start(s32[1,256,32]{1,2,0:T(8,128)} %param.31) | copy-start | bytes 98308
  316.6 26.5 %copy-start.25 = (s32[64]{0:T(128)S(1)}, s32[64]{0:T(128)}, u32[]{:S(2)}) copy-start(s32[64]{0:T(128)} %copy-done.24) | copy-start | bytes 772
  316.6 20.6 %collective-permute-start.11 = (bf16[2048,256]{1,0:T(8,128)(2,1)S(1)}, bf16[2048,256]{1,0:T(8,128)(2,1)S(1)}, u32[]{:S(2)}, u32[]{:S(2)}) collective-permute-start(bf16[2048,256]{1,0:T(8,128)(2,1)S(1)} %broadcast_select_fusion.2), channel_id=1, source_target_pairs={{0,64},{64,128},{128,192},{192,256},{256,320},{320,384},{384,448},... | collective-permute-start | bytes 3145736 | tf_op jit(solution)/shard_map/ppermute | solution.py:13
  321.0 11.8 %collective-permute-start = (bf16[2048]{0:T(1024)(128)(2,1)S(1)}, bf16[2048]{0:T(1024)(128)(2,1)S(1)}, u32[]{:S(2)}, u32[]{:S(2)}) collective-permute-start(bf16[2048]{0:T(1024)(128)(2,1)S(1)} %get-tuple-element.72), channel_id=1, source_target_pairs={{0,64},{64,128},{128,192},{192,256},{256,320},{320,384},{384,448},... | collective-permute-start | bytes 12296 | tf_op jit(solution)/shard_map/ppermute | solution.py:13
  332.8 6.8 %collective-permute-start.1 = (bf16[2048]{0:T(1024)(128)(2,1)S(1)}, bf16[2048]{0:T(1024)(128)(2,1)S(1)}, u32[]{:S(2)}, u32[]{:S(2)}) collective-permute-start(bf16[2048]{0:T(1024)(128)(2,1)S(1)} %convert_maximum_fusion.5), channel_id=1, source_target_pairs={{0,64},{64,128},{128,192},{192,256},{256,320},{320,384},{384,448},... | collective-permute-start | bytes 12296 | tf_op jit(solution)/shard_map/ppermute | solution.py:13
  337.7 30.3 %collective-permute-start.12 = (bf16[2048,256]{1,0:T(8,128)(2,1)S(1)}, bf16[2048,256]{1,0:T(8,128)(2,1)}, u32[]{:S(2)}, u32[]{:S(2)}) collective-permute-start(bf16[2048,256]{1,0:T(8,128)(2,1)S(1)} %broadcast_select_fusion.1), channel_id=1, source_target_pairs={{0,64},{64,128},{128,192},{192,256},{256,320},{320,384},{384,448},... | collective-permute-start | bytes 3145736 | tf_op jit(solution)/shard_map/ppermute | solution.py:13
  339.7 11.7 %collective-permute-start.2 = (bf16[2048]{0:T(1024)(128)(2,1)S(1)}, bf16[2048]{0:T(1024)(128)(2,1)S(1)}, u32[]{:S(2)}, u32[]{:S(2)}) collective-permute-start(bf16[2048]{0:T(1024)(128)(2,1)S(1)} %convert_maximum_fusion.4), channel_id=1, source_target_pairs={{0,64},{64,128},{128,192},{192,256},{256,320},{320,384},{384,448},... | collective-permute-start | bytes 12296 | tf_op jit(solution)/shard_map/ppermute | solution.py:13
  352.0 13.3 %collective-permute-start.3 = (bf16[2048]{0:T(1024)(128)(2,1)}, bf16[2048]{0:T(1024)(128)(2,1)}, u32[]{:S(2)}, u32[]{:S(2)}) collective-permute-start(bf16[2048]{0:T(1024)(128)(2,1)} %convert_maximum_fusion.3), channel_id=1, source_target_pairs={{0,64},{64,128},{128,192},{192,256},{256,320},{320,384},{384,448},... | collective-permute-start | bytes 12296 | tf_op jit(solution)/shard_map/ppermute | solution.py:13
  365.3 8.4 %copy-start.11 = (s32[1,256,32]{2,1,0:T(8,128)S(1)}, s32[1,256,32]{2,1,0:T(8,128)}, u32[]{:S(2)}) copy-start(s32[1,256,32]{2,1,0:T(8,128)} %copy.47) | copy-start | bytes 98308
  365.3 8.5 %copy-start.12 = (s32[1,256,32]{2,1,0:T(8,128)S(1)}, s32[1,256,32]{2,1,0:T(8,128)}, u32[]{:S(2)}) copy-start(s32[1,256,32]{2,1,0:T(8,128)} %copy.49) | copy-start | bytes 98308
  365.3 8.5 %copy-start.13 = (s32[256,32]{1,0:T(8,128)S(1)}, s32[256,32]{1,0:T(8,128)}, u32[]{:S(2)}) copy-start(s32[256,32]{1,0:T(8,128)} %copy.56) | copy-start | bytes 98308
  365.3 8.5 %copy-start.23 = (s32[4,64]{1,0:T(4,128)S(1)}, s32[4,64]{1,0:T(4,128)}, u32[]{:S(2)}) copy-start(s32[4,64]{1,0:T(4,128)} %sub.46) | copy-start | bytes 3076
  366.0 7.8 %collective-permute-start.4 = (bf16[2048]{0:T(1024)(128)(2,1)S(1)}, bf16[2048]{0:T(1024)(128)(2,1)S(1)}, u32[]{:S(2)}, u32[]{:S(2)}) collective-permute-start(bf16[2048]{0:T(1024)(128)(2,1)S(1)} %convert_maximum_fusion.2), channel_id=1, source_target_pairs={{0,64},{64,128},{128,192},{192,256},{256,320},{320,384},{384,448},... | collective-permute-start | bytes 12296 | tf_op jit(solution)/shard_map/ppermute | solution.py:13
  370.2 25.5 %collective-permute-start.13 = (bf16[2048,256]{1,0:T(8,128)(2,1)}, bf16[2048,256]{1,0:T(8,128)(2,1)}, u32[]{:S(2)}, u32[]{:S(2)}) collective-permute-start(bf16[2048,256]{1,0:T(8,128)(2,1)} %broadcast_select_fusion), channel_id=1, source_target_pairs={{0,64},{64,128},{128,192},{192,256},{256,320},{320,384},{384,448},... | collective-permute-start | bytes 3145736 | tf_op jit(solution)/shard_map/ppermute | solution.py:13
  373.9 11.9 %collective-permute-start.5 = (bf16[2048]{0:T(1024)(128)(2,1)S(1)}, bf16[2048]{0:T(1024)(128)(2,1)S(1)}, u32[]{:S(2)}, u32[]{:S(2)}) collective-permute-start(bf16[2048]{0:T(1024)(128)(2,1)S(1)} %convert_maximum_fusion.1), channel_id=1, source_target_pairs={{0,64},{64,128},{128,192},{192,256},{256,320},{320,384},{384,448},... | collective-permute-start | bytes 12296 | tf_op jit(solution)/shard_map/ppermute | solution.py:13
  385.8 5.6 %collective-permute-start.6 = (bf16[2048]{0:T(1024)(128)(2,1)S(1)}, bf16[2048]{0:T(1024)(128)(2,1)S(1)}, u32[]{:S(2)}, u32[]{:S(2)}) collective-permute-start(bf16[2048]{0:T(1024)(128)(2,1)S(1)} %convert_maximum_fusion), channel_id=1, source_target_pairs={{0,64},{64,128},{128,192},{192,256},{256,320},{320,384},{384,448},... | collective-permute-start | bytes 12296 | tf_op jit(solution)/shard_map/ppermute | solution.py:13
  395.8 6.6 %copy-start.16 = (bf16[256,256]{1,0:T(8,128)(2,1)S(1)}, bf16[256,256]{1,0:T(8,128)(2,1)}, u32[]{:S(2)}) copy-start(bf16[256,256]{1,0:T(8,128)(2,1)} %param.45) | copy-start | bytes 393220
  395.8 7.4 %copy-start.2 = (bf16[384,512]{1,0:T(8,128)(2,1)S(1)}, bf16[384,512]{1,0:T(8,128)(2,1)}, u32[]{:S(2)}) copy-start(bf16[384,512]{1,0:T(8,128)(2,1)} %param.46) | copy-start | bytes 1179652
  403.2 115.4 %copy-start.27 = (f32[256]{0:T(256)S(1)}, f32[256]{0:T(256)}, u32[]{:S(2)}) copy-start(f32[256]{0:T(256)} %param.50) | copy-start | bytes 3076
  403.2 115.4 %copy-start.28 = (bf16[256,1]{0,1:T(2,128)(2,1)S(1)}, bf16[256,1]{0,1:T(2,128)(2,1)}, u32[]{:S(2)}) copy-start(bf16[256,1]{0,1:T(2,128)(2,1)} %reshape.541) | copy-start | bytes 1540
  403.2 9.5 %copy-start.7 = (s32[4,64,32]{2,1,0:T(8,128)}, s32[4,64,32]{2,1,0:T(8,128)S(1)}, u32[]{:S(2)}) copy-start(s32[4,64,32]{2,1,0:T(8,128)S(1)} %get-tuple-element.170) | copy-start | bytes 98308 | tf_op jit(solution)/shard_map/while
  403.2 9.5 %copy-start.9 = (s32[4,64,32]{2,1,0:T(8,128)}, s32[4,64,32]{2,1,0:T(8,128)S(1)}, u32[]{:S(2)}) copy-start(s32[4,64,32]{2,1,0:T(8,128)S(1)} %get-tuple-element.173) | copy-start | bytes 98308 | tf_op jit(solution)/shard_map/while
  427.4 4.0 copy-start.3
  427.4 4.0 copy-start.8
  427.4 4.0 copy-start.10
  431.4 9.5 %copy-start.7 = (s32[4,64,32]{2,1,0:T(8,128)}, s32[4,64,32]{2,1,0:T(8,128)S(1)}, u32[]{:S(2)}) copy-start(s32[4,64,32]{2,1,0:T(8,128)S(1)} %get-tuple-element.170) | copy-start | bytes 98308 | tf_op jit(solution)/shard_map/while
  431.4 9.5 %copy-start.9 = (s32[4,64,32]{2,1,0:T(8,128)}, s32[4,64,32]{2,1,0:T(8,128)S(1)}, u32[]{:S(2)}) copy-start(s32[4,64,32]{2,1,0:T(8,128)S(1)} %get-tuple-element.173) | copy-start | bytes 98308 | tf_op jit(solution)/shard_map/while
  455.6 4.0 copy-start.3
  455.6 4.0 copy-start.8
  455.6 4.0 copy-start.10
  459.6 9.5 %copy-start.7 = (s32[4,64,32]{2,1,0:T(8,128)}, s32[4,64,32]{2,1,0:T(8,128)S(1)}, u32[]{:S(2)}) copy-start(s32[4,64,32]{2,1,0:T(8,128)S(1)} %get-tuple-element.170) | copy-start | bytes 98308 | tf_op jit(solution)/shard_map/while
  459.6 9.5 %copy-start.9 = (s32[4,64,32]{2,1,0:T(8,128)}, s32[4,64,32]{2,1,0:T(8,128)S(1)}, u32[]{:S(2)}) copy-start(s32[4,64,32]{2,1,0:T(8,128)S(1)} %get-tuple-element.173) | copy-start | bytes 98308 | tf_op jit(solution)/shard_map/while
  483.8 4.0 copy-start.3
  483.8 4.0 copy-start.8
  483.8 4.0 copy-start.10
  487.8 9.5 %copy-start.7 = (s32[4,64,32]{2,1,0:T(8,128)}, s32[4,64,32]{2,1,0:T(8,128)S(1)}, u32[]{:S(2)}) copy-start(s32[4,64,32]{2,1,0:T(8,128)S(1)} %get-tuple-element.170) | copy-start | bytes 98308 | tf_op jit(solution)/shard_map/while
  487.8 9.5 %copy-start.9 = (s32[4,64,32]{2,1,0:T(8,128)}, s32[4,64,32]{2,1,0:T(8,128)S(1)}, u32[]{:S(2)}) copy-start(s32[4,64,32]{2,1,0:T(8,128)S(1)} %get-tuple-element.173) | copy-start | bytes 98308 | tf_op jit(solution)/shard_map/while
  512.0 4.0 copy-start.3
  512.0 4.0 copy-start.8
  512.0 4.1 copy-start.10
  (1 other events, 0.9 us)
where the time goes:
time: 524 us; the launch traced here: 522 us
  waiting for transfers between devices  260 us (50%)
  local copies, waits for them, and re-layouts  91.4 us (17%)
  starting transfers between devices  80.8 us (15%)
  matrix products  57.2 us (11%)
  other arithmetic  31 us (6%)
    all_to_all x1, waiting for transfers between devices, shards(): lax.all_to_all(tile_block, 'dom', split_axis=0, concat_axis=0, tiled=True)  173 us
    ppermute x14, waiting for transfers between devices, passed_along(): lax.ppermute(value, axis, [(source, source + steps) for source in range(f...  73.8 us
    ppermute x14, starting transfers between devices, passed_along(): lax.ppermute(value, axis, [(source, source + steps) for source in range(f...  55.6 us
    gather x4, local copies, waits for them, and re-layouts, attend(): neighbour_mem = fetched_rows[rows_block.reshape(-1)]  37.5 us
    dot_general x4, matrix products, attend(): jnp.dot(neighbour_code, keyval_weight[mem_width:], preferred_element_type...  26.6 us
    all_to_all x1, starting transfers between devices, shards(): lax.all_to_all(wanted.reshape(owners, 1), 'dom', split_axis=0, concat_axi...  19.3 us
    all_to_all x1, waiting for transfers between devices, shards(): lax.all_to_all(wanted.reshape(owners, 1), 'dom', split_axis=0, concat_axi...  13.2 us
    squeeze x4, local copies, waits for them, and re-layouts, attend(): value_heads = keyval[:, :, 1]  10.7 us
  transfers between devices with their start and end apart: 16, of which 9 were waited for; matrix products, arithmetic and copies ran while one was open for 5% of the time, Pallas kernels for 0%

commit v1 on v0

v1 whole, which is shorter than its diff:
```python
import jax
import jax.numpy as jnp
from jax import lax
from jax.experimental import pallas as pl
from jax.experimental.pallas import tpu as pltpu
from jax.sharding import Mesh, PartitionSpec as P

HEADS = 2
TILE = 128
PLANE = ("x", "c", "y", "zp")
VMEM = pl.BlockSpec(memory_space=pltpu.VMEM)
SMEM = pl.BlockSpec(memory_space=pltpu.SMEM)
F32 = jnp.float32
BF16 = jnp.bfloat16


def params(mib):
    return pltpu.CompilerParams(vmem_limit_bytes=mib * 2**20)


def dot(a, b):
    return jnp.dot(a, b, preferred_element_type=F32)


def time_code(delta, time_freq, time_phase):
    angle = delta.astype(F32)[..., None] * time_freq + time_phase
    return jnp.cos(angle).astype(BF16)


def select_kernel(req_ref, ring_ref, left_ref, right_ref):
    dests, blocks = left_ref.shape[:2]
    half = left_ref.shape[3]

    def body(dest, carry):
        for block in range(blocks):
            tile = req_ref[dest * blocks + block]
            left_ref[dest, block] = ring_ref[block, tile, :, :half]
            right_ref[dest, block] = ring_ref[block, tile, :, half:]
        return carry

    lax.fori_loop(0, dests, body, 0)


def select_tiles(requests, ring):
    blocks, _, rows, width = ring.shape
    dests = requests.shape[0]
    out = jax.ShapeDtypeStruct((dests, blocks, rows, width // 2), ring.dtype)
    return pl.pallas_call(
        select_kernel,
        out_shape=(out, out),
        in_specs=[SMEM, VMEM],
        out_specs=(VMEM, VMEM),
        compiler_params=params(40),
        cost_estimate=pl.CostEstimate(flops=0, bytes_accessed=6 * 2**20, transcendentals=0),
    )(requests.reshape(-1), ring)


def gather_rows(index_ref, table, out, count, unroll=32):
    def body(step, carry):
        first = pl.multiple_of(step * unroll, unroll)
        for lane in range(unroll):
            row = index_ref[first + lane]
            out[pl.ds(first + lane, 1), :] = table[pl.ds(row, 1), :]
        return carry

    lax.fori_loop(0, count // unroll, body, 0)


def widen(source_ref, wide, chunk=512):
    def body(step, carry):
        at = pl.ds(pl.multiple_of(step * chunk, chunk), chunk)
        wide[at, :] = source_ref[at, :].astype(F32)
        return carry

    lax.fori_loop(0, wide.shape[0] // chunk, body, 0)


def gather_kernel(index_ref, table_ref, out_ref, wide, picked):
    count = out_ref.shape[0]
    widen(table_ref, wide)
    gather_rows(index_ref, wide, picked, count)

    def body(step, carry):
        at = pl.ds(pl.multiple_of(step * 512, 512), 512)
        out_ref[at, :] = picked[at, :].astype(BF16)
        return carry

    lax.fori_loop(0, count // 512, body, 0)


def gather_half(index, table):
    count = index.shape[0]
    rows, width = table.shape
    return pl.pallas_call(
        gather_kernel,
        out_shape=jax.ShapeDtypeStruct((count, width), BF16),
        in_specs=[SMEM, VMEM],
        out_specs=VMEM,
        scratch_shapes=[pltpu.VMEM((rows, width), F32), pltpu.VMEM((count, width), F32)],
        compiler_params=params(40),
        cost_estimate=pl.CostEstimate(flops=0, bytes_accessed=30 * 2**20, transcendentals=0),
    )(index, table)


def update_kernel(index_ref, table_ref, left_ref, base_ref, hid_ref, same_ref, source_ref, weight_ref, written_ref, right_ref, wide, picked):
    events, half = left_ref.shape[0] // 2, left_ref.shape[1]
    width = 2 * half
    widen(table_ref, wide)
    gather_rows(index_ref, wide, picked, 2 * events)
    right_ref[...] = picked[...].astype(BF16)
    target = jnp.concatenate([left_ref[:events, :], right_ref[:events, :]], axis=1)
    pre = base_ref[...] + dot(target, weight_ref[...])
    same = same_ref[...]
    tally = jnp.sum(same, axis=1, keepdims=True)
    summed = jnp.dot(same, pre, preferred_element_type=F32, precision=lax.Precision.HIGHEST)
    gate_in = summed / tally
    hid = hid_ref[...]
    reset = jax.nn.sigmoid(gate_in[:, :width] + hid[:, :width])
    keep = jax.nn.sigmoid(gate_in[:, width : 2 * width] + hid[:, width : 2 * width])
    cand = jnp.tanh(gate_in[:, 2 * width :] + reset * hid[:, 2 * width :])
    state = source_ref[...].astype(F32)
    written_ref[...] = ((1.0 - keep) * cand + keep * state).astype(BF16)


def update_rows(index, table, left, base, hid, same, source, weight):
    events, width = source.shape
    rows, half = table.shape
    return pl.pallas_call(
        update_kernel,
        out_shape=(
            jax.ShapeDtypeStruct((events, width), BF16),
            jax.ShapeDtypeStruct((2 * events, half), BF16),
        ),
        in_specs=[SMEM] + [VMEM] * 7,
        out_specs=(VMEM, VMEM),
        scratch_shapes=[pltpu.VMEM((rows, half), F32), pltpu.VMEM((2 * events, half), F32)],
        compiler_params=params(40),
        cost_estimate=pl.CostEstimate(flops=10**9, bytes_accessed=12 * 2**20, transcendentals=0),
    )(index, table, left, base, hid, same, source, weight)


def keyval_kernel(index_ref, table_ref, left_ref, code_ref, weight_ref, out_ref, wide, picked):
    count = out_ref.shape[0]
    widen(table_ref, wide)
    gather_rows(index_ref, wide, picked, count)
    weight = weight_ref[...]

    def body(step, carry):
        at = pl.ds(pl.multiple_of(step * 256, 256), 256)
        joined = jnp.concatenate(
            [left_ref[at, :], picked[at, :].astype(BF16), code_ref[at, :]], axis=1
        )
        out_ref[at, :] = dot(joined, weight).astype(BF16)
        return carry

    lax.fori_loop(0, count // 256, body, 0)


def keyval_rows(index, table, left, code, weight):
    count = index.shape[0]
    rows, half = table.shape
    return pl.pallas_call(
        keyval_kernel,
        out_shape=jax.ShapeDtypeStruct((count, weight.shape[1]), BF16),
        in_specs=[SMEM] + [VMEM] * 4,
        out_specs=VMEM,
        scratch_shapes=[pltpu.VMEM((rows, half), F32), pltpu.VMEM((count, half), F32)],
        compiler_params=params(48),
        cost_estimate=pl.CostEstimate(
            flops=2 * count * weight.shape[0] * weight.shape[1],
            bytes_accessed=40 * 2**20,
            transcendentals=0,
        ),
    )(index, table, left, code, weight)


def attend_kernel(
    latest_ref,
    rows_ref,
    source_ref,
    query_ref,
    keyval_ref,
    left_ref,
    right_ref,
    out_weight_ref,
    bias_out_ref,
    pred_ref,
    bias_pred_ref,
    logit_ref,
    logits_ref,
    queries,
    attended,
):
    events, width = source_ref.shape
    head = width // HEADS
    neighbours = keyval_ref.shape[0] // events
    latest = latest_ref[...]
    lanes = lax.broadcasted_iota(jnp.int32, (events, TILE), 1)
    hot = jnp.concatenate(
        [
            (latest == lanes + first).astype(F32).astype(BF16)
            for first in range(0, rows_ref.shape[0], TILE)
        ],
        axis=1,
    )
    moved = dot(hot, rows_ref[...])
    known = jnp.concatenate([latest] * HEADS, axis=1) >= 0
    current = jnp.where(known, moved, source_ref[...].astype(F32)).astype(BF16)
    queries[...] = dot(current, query_ref[...]).astype(BF16).astype(F32)
    group = 8
    columns = group * neighbours
    owner = lax.broadcasted_iota(jnp.int32, (HEADS * group, columns), 1) // neighbours
    event = lax.broadcasted_iota(jnp.int32, (HEADS * group, columns), 0) % group
    own = owner == event
    low = lax.broadcasted_iota(jnp.int32, (group, width), 1) < head
    scale = 1.0 / jnp.sqrt(F32(head))

    def body(step, carry):
        at = pl.ds(pl.multiple_of(step * columns, columns), columns)
        mine = pl.ds(pl.multiple_of(step * group, group), group)
        block = queries[mine, :]
        zero = jnp.zeros_like(block)
        stacked = jnp.concatenate(
            [jnp.where(low, block, zero), jnp.where(low, zero, block)], axis=0
        ).astype(BF16)
        keys = keyval_ref[at, :width]
        scores = lax.dot_general(
            stacked, keys, (((1,), (1,)), ((), ())), preferred_element_type=F32
        )
        scores = jnp.where(own, scores * scale, -jnp.inf)
        top = jnp.max(scores, axis=1, keepdims=True)
        exponent = jnp.exp(scores - top)
        weights = (exponent / jnp.sum(exponent, axis=1, keepdims=True)).astype(BF16)
        mixed = dot(weights, keyval_ref[at, width:])
        attended[mine, :] = jnp.where(low, mixed[:group, :], mixed[group:, :])
        return carry

    lax.fori_loop(0, events // group, body, 0)
    embedding = dot(attended[...].astype(BF16), out_weight_ref[:width, :])
    embedding = embedding + dot(current, out_weight_ref[width:, :]) + bias_out_ref[...]
    embedding = jnp.maximum(embedding, 0.0).astype(BF16)
    embed_part = dot(embedding, pred_ref[:width, :])
    other = jnp.concatenate([left_ref[...], right_ref[...]], axis=1)
    other_part = dot(other, pred_ref[width:, :])
    for side in range(2):
        hidden = embed_part + other_part[side * events : (side + 1) * events, :]
        hidden = jnp.maximum(hidden + bias_pred_ref[...], 0.0).astype(BF16)
        logits_ref[side : side + 1, :] = lax.dot_general(
            logit_ref[...], hidden, (((1,), (1,)), ((), ())), preferred_element_type=F32
        )


def attend(latest, rows, source, query_weight, keyval, left, right, out_weight, bias_out, pred_weight, bias_pred, logit_weight):
    events, width = source.shape
    return pl.pallas_call(
        attend_kernel,
        out_shape=jax.ShapeDtypeStruct((2, events), F32),
        in_specs=[VMEM] * 12,
        out_specs=VMEM,
        scratch_shapes=[pltpu.VMEM((events, width), F32), pltpu.VMEM((events, width), F32)],
        compiler_params=params(40),
        cost_estimate=pl.CostEstimate(flops=10**9, bytes_accessed=12 * 2**20, transcendentals=0),
    )(latest, rows, source, query_weight, keyval, left, right, out_weight, bias_out, pred_weight, bias_pred, logit_weight)


def after_kernel(latest_ref, rows_ref, start_ref, out_ref):
    block = 256
    lanes = lax.broadcasted_iota(jnp.int32, (block, TILE), 1)
    rows = rows_ref[...]

    def body(step, carry):
        at = pl.ds(pl.multiple_of(step * block, block), block)
        latest = latest_ref[at, :]
        hot = jnp.concatenate(
            [
                (latest == lanes + first).astype(F32).astype(BF16)
                for first in range(0, rows.shape[0], TILE)
            ],
            axis=1,
        )
        moved = dot(hot, rows)
        known = jnp.concatenate([latest] * (rows.shape[1] // TILE), axis=1) >= 0
        out_ref[at, :] = jnp.where(known, moved, start_ref[at, :].astype(F32)).astype(BF16)
        return carry

    lax.fori_loop(0, out_ref.shape[0] // block, body, 0)


def memory_rows(latest, rows, start):
    return pl.pallas_call(
        after_kernel,
        out_shape=jax.ShapeDtypeStruct(start.shape, BF16),
        in_specs=[VMEM] * 3,
        out_specs=VMEM,
        compiler_params=params(40),
        cost_estimate=pl.CostEstimate(
            flops=2 * start.shape[0] * rows.shape[0] * rows.shape[1],
            bytes_accessed=5 * 2**20,
            transcendentals=0,
        ),
    )(latest, rows, start)


def shards(
    memory_start,
    src_row,
    dst_pos,
    neg_pos,
    nbr_pos,
    event_time,
    nbr_time,
    edge_feat,
    tile_req,
    tile_count,
    time_freq,
    time_phase,
    msg_memory,
    msg_time,
    msg_edge,
    bias_input,
    hid_weight,
    bias_hidden,
    query_weight,
    keyval_weight,
    out_weight,
    bias_out,
    pred_weight,
    bias_pred,
    logit_weight,
):
    nx, nc, ny, nzq, nzp = (lax.axis_size(name) for name in ("x", "c", "y", "zq", "zp"))
    batches = nx * nc
    owners = ny * nzq * nzp
    node_rows, width = memory_start.shape
    half = width // 2
    events = src_row.shape[1]
    neighbours = nbr_pos.shape[2]
    tiles = node_rows // TILE
    share = TILE // batches
    batch = lax.axis_index("x") * nc + lax.axis_index("c")

    own_share = lax.dynamic_index_in_dim(
        memory_start.reshape(tiles, batches, share, width), batch, 1, False
    )
    ring = lax.all_gather(own_share, "zq")
    wanted = tile_req.reshape(ny, nzq, nzp).transpose(0, 2, 1).reshape(1, ny * nzp, nzq)
    wanted = jnp.broadcast_to(wanted, (batches, ny * nzp, nzq)).reshape(-1, nzq)
    asked = lax.all_to_all(wanted, PLANE, 0, 0, tiled=True)
    send_left, send_right = select_tiles(asked, ring)
    left_table = lax.all_to_all(send_left, PLANE, 0, 0, tiled=True).reshape(-1, half)
    right_table = lax.all_to_all(send_right, PLANE, 0, 0, tiled=True).reshape(-1, half)

    running = jnp.cumsum(tile_count.reshape(owners))

    def table_rows(position):
        owner = jnp.sum((running <= (position // TILE)[..., None]).astype(jnp.int32), axis=-1)
        row = position % TILE
        oy, ozq, ozp = owner // (nzq * nzp), (owner // nzp) % nzq, owner % nzp
        source = ((row // share) * ny + oy) * nzp + ozp
        return (source * nzq + ozq) * share + row % share

    dst_rows = table_rows(dst_pos.reshape(events))
    neg_rows = table_rows(neg_pos.reshape(events))
    nbr_rows = table_rows(nbr_pos.reshape(events * neighbours))
    pair_rows = jnp.concatenate([dst_rows, neg_rows])

    sources = src_row.reshape(events)
    event_times = event_time.reshape(events)
    past_times = nbr_time.reshape(events, neighbours)
    ages = event_times[:, None] - past_times
    code = time_code(ages.reshape(-1), time_freq, time_phase)
    source_mem = memory_start[sources]
    base = dot(source_mem, msg_memory[:width])
    base = base + dot(time_code(ages[:, 0], time_freq, time_phase), msg_time)
    base = base + dot(edge_feat.reshape(events, -1), msg_edge)
    base = base + bias_input
    hid = dot(source_mem, hid_weight) + bias_hidden
    same = (sources[:, None] == sources[None, :]).astype(F32)
    all_sources = lax.all_gather(sources, ("x", "c")).reshape(-1)
    order = jnp.arange(batches * events, dtype=jnp.int32)
    of_batch = order // events
    node_ids = jnp.arange(node_rows, dtype=jnp.int32)
    upto = jnp.where(of_batch <= batch, all_sources, -1)
    earlier = jnp.where(of_batch < batch, all_sources, -1)
    after_row = jnp.max(jnp.where(upto[None, :] == node_ids[:, None], order[None, :], -1), axis=1)
    before_row = jnp.max(jnp.where(earlier[None, :] == sources[:, None], order[None, :], -1), axis=1)
    after_row = jnp.broadcast_to(after_row[:, None], (node_rows, TILE))
    before_row = jnp.broadcast_to(before_row[:, None], (events, TILE))

    left_rows = gather_half(jnp.concatenate([nbr_rows, pair_rows]), left_table)
    nbr_left = left_rows[: events * neighbours]
    pair_left = left_rows[events * neighbours :]
    written, pair_right = update_rows(
        pair_rows, right_table, pair_left, base, hid, same, source_mem, msg_memory[width:]
    )
    rows = lax.all_to_all(
        jnp.broadcast_to(written[None], (batches, events, width)), ("x", "c"), 0, 0, tiled=True
    ).reshape(-1, width)
    keyval = keyval_rows(nbr_rows, right_table, nbr_left, code, keyval_weight)
    logits = attend(
        before_row,
        rows,
        source_mem,
        query_weight,
        keyval,
        pair_left,
        pair_right,
        out_weight,
        bias_out.reshape(1, -1),
        pred_weight,
        bias_pred.reshape(1, -1),
        logit_weight.reshape(1, -1),
    )
    memory_after = memory_rows(after_row, rows, memory_start)
    return (logits.reshape(2, 1, events), memory_after.reshape(1, node_rows, width))


def solution(mesh):
    grid = Mesh(mesh.devices.reshape(4, 2, 4, 8, 2), ("x", "c", "y", "zq", "zp"))
    tm, dom = ("x", "c"), ("y", "zq", "zp")
    by_event = [P(tm, dom), P(tm, dom, None)]
    in_specs = (
        P(dom, None),
        by_event[0],
        by_event[0],
        by_event[0],
        by_event[1],
        by_event[0],
        by_event[1],
        by_event[1],
        by_event[1],
        by_event[1],
    ) + (P(),) * 15
    out_specs = (P(None, tm, dom), P(tm, dom, None))
    return jax.shard_map(
        shards, mesh=grid, in_specs=in_specs, out_specs=out_specs, check_vma=False
    )
```

time: 524 us -> 262 us (0.50)
  waiting for transfers between devices: 260 us -> 35.4 us
  blocking collectives: 0 us -> 79.4 us
  starting transfers between devices: 80.8 us -> 8.3 us
  local copies, waits for them, and re-layouts: 91.4 us -> 29.3 us
  Pallas kernels: 0 us -> 57.7 us
  matrix products: 57.2 us -> 3.8 us
  between operations: 1.38 us -> 14.5 us
    all_to_all x2, waiting for transfers between devices: 186 us -> 0.01 us  [the longest x1 0.01 us: shards(): lax.all_to_all(send_right, PLANE, 0, 0, tiled=True).reshape(-1, half)]
    ppermute x14 -> x0, waiting for transfers between devices: 73.8 us -> none  [passed_along(): lax.ppermute(value, axis, [(source, source + steps) for source in range(f...]
    all_to_all x0 -> x2, blocking collectives: none -> 58.7 us  [the longest x1 40.7 us: shards(): lax.all_to_all(send_left, PLANE, 0, 0, tiled=True).reshape(-1, half)]
    pallas_call x0 -> x6, Pallas kernels: none -> 57.7 us  [the longest x1 22.5 us: keyval_rows(): pl.pallas_call(keyval_kernel, out_shape=jax.ShapeDtypeStruct((count, weig...]
    ppermute x14 -> x0, starting transfers between devices: 55.6 us -> none  [passed_along(): lax.ppermute(value, axis, [(source, source + steps) for source in range(f...]
    dot_general x26 -> x4, matrix products: 57.2 us -> 3.8 us  [dot(): return jnp.dot(a, b, preferred_element_type=F32)]
    gather x8 -> x0, local copies, waits for them, and re-layouts: 52.1 us -> none  [the longest x4 37.5 us: attend(): neighbour_mem = fetched_rows[rows_block.reshape(-1)]]
    all_gather x0 -> x1, waiting for transfers between devices: none -> 35.3 us  [shards(): ring = lax.all_gather(own_share, 'zq')]
  transfers between devices with their start and end apart: 16 -> 3, of which waited for: 9 -> 1; matrix products, arithmetic and copies ran while one was open for 5% -> 17% of each run, Pallas kernels for 0% -> 12%
where the time goes in v1:
time: 262 us; the launch traced here: 260 us
  blocking collectives  79.4 us (30%)
  Pallas kernels  57.7 us (22%)
  waiting for transfers between devices  35.4 us (14%)
  other arithmetic  31.5 us (12%)
  local copies, waits for them, and re-layouts  29.3 us (11%)
  between operations  14.5 us (6%)
  starting transfers between devices  8.3 us (3%)
  matrix products  3.8 us (1%)
    all_to_all x1, blocking collectives, shards(): lax.all_to_all(send_left, PLANE, 0, 0, tiled=True).reshape(-1, half)  40.7 us
    all_gather x1, waiting for transfers between devices, shards(): ring = lax.all_gather(own_share, 'zq')  35.3 us
    pallas_call x1, Pallas kernels, keyval_rows(): pl.pallas_call(keyval_kernel, out_shape=jax.ShapeDtypeStruct((count, weig...  22.5 us
    all_gather x1, blocking collectives, shards(): all_sources = lax.all_gather(sources, ('x', 'c')).reshape(-1)  20.7 us
    all_to_all x1, blocking collectives, shards(): asked = lax.all_to_all(wanted, PLANE, 0, 0, tiled=True)  18 us
    unnamed x80, local copies, waits for them, and re-layouts  18 us
    convert_element_type x1, other arithmetic, time_code(): return jnp.cos(angle).astype(BF16)  16.9 us
    pallas_call x1, Pallas kernels, attend(): pl.pallas_call(attend_kernel, out_shape=jax.ShapeDtypeStruct((2, events),...  16.3 us
  transfers between devices with their start and end apart: 3, of which 1 were waited for; matrix products, arithmetic and copies ran while one was open for 17% of the time, Pallas kernels for 12%

profile of v1, /device:TPU:1, one launch (start us, length us, event | category | flops | bytes accessed | tf_op | source)
XLA Modules:
  0.0 259.8 jit_solution(7678358216114129764)
XLA Ops:
  7.2 1.6 constant_dynamic-slice_fusion
  8.9 0.5 broadcast.338
  9.4 1.3 reduce.7
  10.7 0.1 reshape.260
  10.8 0.1 copy.45
  10.9 18.0 %all_to_all.24 = s32[64,1,8]{2,1,0:T(1,128)S(1)} all-to-all(s32[64,1,8]{2,1,0:T(1,128)S(1)} %bitcast.42), channel_id=1, replica_groups=mesh['x'=4,'c'=2,'y'=4,'zq'=8,'zp'=2] {'x','c','y','zp'}, dimensions={0} | all-to-all | bytes 4096 | tf_op jit(solution)/shard_map/all_to_all | solution.py:348
  28.9 0.7 reduce.8
  29.8 35.3 %all-gather.4.cloned.1.call-done = bf16[128,1,16,256]{3,2,1,0:T(8,128)(2,1)} async-done(((bf16[16,1,16,256]{3,2,1,0:T(8,128)(2,1)}), bf16[128,1,16,256]{3,2,1,0:T(8,128)(2,1)}) %all-gather.4.cloned.1.call-update) | async-done | bytes 1048592 | tf_op jit(solution)/shard_map/all_gather | solution.py:345
  65.1 1.2 copy-done.13
  66.3 1.9 shard_map.248
  68.2 40.7 %all_to_all.25 = bf16[64,8,16,128]{3,2,1,0:T(8,128)(2,1)} all-to-all(bf16[64,8,16,128]{3,2,1,0:T(8,128)(2,1)S(1)} %get-tuple-element.7), channel_id=1, replica_groups=mesh['x'=4,'c'=2,'y'=4,'zq'=8,'zp'=2] {'x','c','y','zp'}, dimensions={0} | all-to-all | bytes 4194304 | tf_op jit(solution)/shard_map/all_to_all | solution.py:350
  108.9 4.4 %all-to-all-start.1 = ((bf16[64,8,16,128]{3,2,1,0:T(8,128)(2,1)}), bf16[64,8,16,128]{3,2,1,0:T(8,128)(2,1)S(1)}, u32[]{:S(2)}, u32[]{:S(2)}) async-start(bf16[64,8,16,128]{3,2,1,0:T(8,128)(2,1)} %copy-done.7), calls=%async_computation.1 | async-start | bytes 4194304 | tf_op jit(solution)/shard_map/all_to_all | solution.py:351
  113.4 0.1 copy.44
  113.5 0.1 reduce-window.8
  113.6 0.1 reduce
  113.7 0.1 copy.46
  113.8 0.7 reshape.264
  114.5 2.3 gather_fusion
  116.9 0.8 slice.18.weight_ref
  117.8 0.7 sub.95
  118.4 0.9 copy.48
  119.3 0.7 reshape.270
  120.0 0.7 reshape.273.logit_ref
  120.7 20.7 %all-gather.1 = s32[8,1,256]{2,1,0:T(1,128)S(1)} all-gather(s32[1,1,256]{2,1,0:T(1,128)S(1)} %bitcast.47), channel_id=1, replica_groups=mesh['x'=4,'c'=2,'y'=4,'zq'=8,'zp'=2] {'x','c'}, dimensions={0}, use_global_device_ids=true | all-gather | bytes 9216 | tf_op jit(solution)/shard_map/all_gather | solution.py:379
  141.4 0.7 and_select_fusion.13
  142.0 0.7 and_select_fusion.5
  142.8 0.7 fusion.35
  143.6 0.8 add_select_fusion.5
  144.4 0.3 convert_reduce_fusion
  144.7 0.7 fusion.40
  145.4 0.6 fusion.30
  146.0 0.9 fusion.14.index_ref
  146.9 0.6 copy-done.15
  147.5 0.8 subtract_convert_fusion
  148.3 1.6 compare_convert_fusion.same_ref
  149.8 0.3 fusion.1
  150.1 1.0 convolution_add_fusion.hid_ref
  151.1 1.4 convolution_add_fusion.2
  152.5 1.2 fusion.base_ref
  153.7 16.9 %cosine_convert_fusion.code_ref = bf16[8192,128]{1,0:T(8,128)(2,1)} fusion(f32[128]{0:T(128)S(1)} %copy-done.35, f32[128]{0:T(128)S(1)} %copy-done.36, f32[8192]{0:T(1024)S(1)} %subtract_convert_fusion), kind=kLoop, calls=%fused_computation.3 | loop fusion | flops 3145728 | bytes 2130944 | tf_op jit(solution)/shard_map/convert_element_type | solution.py:27
  170.6 9.9 %shard_map.249 = bf16[8704,128]{1,0:T(8,128)(2,1)S(1)} custom-call(s32[8704]{0:T(1024)S(1)} %pad_add_fusion.index_ref, bf16[8192,128]{1,0:T(8,128)(2,1)S(1)} %bitcast.34), custom_call_target="tpu_custom_call" | custom-call | bytes 31457280 | tf_op jit(solution)/shard_map/pallas_call | solution.py:94
  180.5 1.4 copy-done.2
  181.9 1.2 copy-done.6
  183.1 1.0 copy-done.8
  184.1 0.9 copy-done.12
  185.0 2.5 shard_map.250
  187.6 0.6 copy-done.20
  188.2 1.0 broadcast_in_dim.42
  189.3 3.9 %all-to-all-start.3 = ((bf16[8,256,256]{2,1,0:T(8,128)(2,1)}), bf16[8,256,256]{2,1,0:T(8,128)(2,1)S(1)}, u32[]{:S(2)}, u32[]{:S(2)}) async-start(bf16[8,256,256]{2,1,0:T(8,128)(2,1)} %broadcast_in_dim.42), calls=%async_computation.3 | async-start | bytes 2097152 | tf_op jit(solution)/shard_map/all_to_all | solution.py:396
  193.1 1.0 select_reduce_fusion.1
  194.1 3.6 %select_reduce_fusion = s32[2048]{0:T(1024)} fusion(s32[2048]{0:T(1024)} %get-tuple-element.20), kind=kLoop, calls=%fused_computation.1 | loop fusion | flops 12580864 | bytes 16384 | tf_op jit(solution)/shard_map/reduce_max | solution.py:385
  197.7 1.8 slice.24.left_ref
  199.5 22.5 %shard_map.251.keyval_ref = bf16[8192,512]{1,0:T(8,128)(2,1)} custom-call(s32[8192]{0:T(1024)S(1)} %copy-done.16, bf16[8192,128]{1,0:T(8,128)(2,1)S(1)} %bitcast.33, bf16[8192,128]{1,0:T(8,128)(2,1)S(1)} %slice.24.left_ref, bf16[8192,128]{1,0:T(8,128)(2,1)} %cosine_convert_fusion.code_ref, bf16[384,512]{1,0:T(8,128)(2,1)S(1)} %copy-done.14), custom_call_target="tpu_custom_call" | custom-call | flops 3221225472 | bytes 41943040 | tf_op jit(solution)/shard_map/pallas_call | solution.py:162
  222.2 3.4 %copy-done.1 = bf16[8192,512]{1,0:T(8,128)(2,1)S(1)} copy-done((bf16[8192,512]{1,0:T(8,128)(2,1)S(1)}, bf16[8192,512]{1,0:T(8,128)(2,1)}, u32[]{:S(2)}) %copy-start.1) | copy-done | bytes 8388632
  225.5 0.9 copy-done.5
  226.4 0.9 copy-done.11
  227.3 0.9 copy-done.17
  228.3 0.9 copy-done.18
  229.2 0.9 copy-done.19
  230.1 0.9 copy-done.21
  231.1 16.3 %shard_map.252 = f32[2,256]{1,0:T(2,128)S(1)} custom-call(s32[256,128]{1,0:T(8,128)S(1)} %broadcast_in_dim.35.latest_ref, bf16[2048,256]{1,0:T(8,128)(2,1)S(1)} %bitcast.35, bf16[256,256]{1,0:T(8,128)(2,1)S(1)} %copy-done.5, bf16[256,256]{1,0:T(8,128)(2,1)S(1)} %copy-done.19, bf16[8192,512]{1,0:T(8,128)(2,1)S(1)} %copy-done.1, ...), custom_call_target="tpu_custom_call" | custom-call | flops 1000000000 | bytes 12582912 | tf_op jit(solution)/shard_map/pallas_call | solution.py:255
  247.3 0.6 copy.49
  247.9 0.3 broadcast_in_dim.45.latest_ref
  248.3 4.7 %shard_map.253 = bf16[2048,256]{1,0:T(8,128)(2,1)} custom-call(s32[2048,128]{1,0:T(8,128)S(1)} %broadcast_in_dim.45.latest_ref, bf16[2048,256]{1,0:T(8,128)(2,1)S(1)} %bitcast.36, bf16[2048,256]{1,0:T(8,128)(2,1)S(1)} %copy-done.9), custom_call_target="tpu_custom_call" | custom-call | flops 2147483648 | bytes 5242880 | tf_op jit(solution)/shard_map/pallas_call | solution.py:290
  (76 shorter events, 0.6 us)
Async XLA Ops:
  7.2 142.9 %copy-start = (bf16[256,768]{1,0:T(8,128)(2,1)S(1)}, bf16[256,768]{1,0:T(8,128)(2,1)}, u32[]{:S(2)}) copy-start(bf16[256,768]{1,0:T(8,128)(2,1)} %param.41) | copy-start | bytes 1179652
  7.2 57.9 %all-gather.4.cloned.1.call-start = ((), (), s32[]{:S(2)}) async-start(), calls=%async_computation.4 | async-start | bytes 1179648 | tf_op jit(solution)/shard_map/all_gather | solution.py:345
  65.1 1.2 copy-start.13
  68.2 40.7 %copy-start.7 = (bf16[64,8,16,128]{3,2,1,0:T(8,128)(2,1)}, bf16[64,8,16,128]{3,2,1,0:T(8,128)(2,1)S(1)}, u32[]{:S(2)}) copy-start(bf16[64,8,16,128]{3,2,1,0:T(8,128)(2,1)S(1)} %get-tuple-element.6) | copy-start | bytes 6291460
  108.9 4.5 %copy-start.37 = (s32[1,1,64]{2,1,0:T(1,128)S(1)}, s32[1,1,64]{2,1,0:T(1,128)}, u32[]{:S(2)}) copy-start(s32[1,1,64]{2,1,0:T(1,128)} %param.34) | copy-start | bytes 772
  108.9 4.8 %copy-start.28 = (s32[1,256,32]{1,2,0:T(8,128)S(1)}, s32[1,256,32]{1,2,0:T(8,128)}, u32[]{:S(2)}) copy-start(s32[1,256,32]{1,2,0:T(8,128)} %param.29) | copy-start | bytes 98308
  108.9 5.6 %copy-start.29 = (s32[1,256]{1,0:T(1,128)S(1)}, s32[1,256]{1,0:T(1,128)}, u32[]{:S(2)}) copy-start(s32[1,256]{1,0:T(1,128)} %param.26) | copy-start | bytes 3076
  108.9 7.9 %copy-start.24 = (bf16[512,768]{1,0:T(8,128)(2,1)S(1)}, bf16[512,768]{1,0:T(8,128)(2,1)}, u32[]{:S(2)}) copy-start(bf16[512,768]{1,0:T(8,128)(2,1)} %param.37) | copy-start | bytes 2359300
  108.9 73.0 %all-to-all-start.1 = ((bf16[64,8,16,128]{3,2,1,0:T(8,128)(2,1)}), bf16[64,8,16,128]{3,2,1,0:T(8,128)(2,1)S(1)}, u32[]{:S(2)}, u32[]{:S(2)}) async-start(bf16[64,8,16,128]{3,2,1,0:T(8,128)(2,1)} %copy-done.7), calls=%async_computation.1 | async-start | bytes 4194304 | tf_op jit(solution)/shard_map/all_to_all | solution.py:351
  113.3 4.3 %copy-start.33 = (s32[1,256]{1,0:T(1,128)S(1)}, s32[1,256]{1,0:T(1,128)}, u32[]{:S(2)}) copy-start(s32[1,256]{1,0:T(1,128)} %param.30) | copy-start | bytes 3076
  116.8 65.1 %copy-start.4 = (bf16[256,256]{1,0:T(8,128)(2,1)}, bf16[256,256]{1,0:T(8,128)(2,1)S(1)}, u32[]{:S(2)}) copy-start(bf16[256,256]{1,0:T(8,128)(2,1)S(1)} %gather_fusion) | copy-start | bytes 393220
  120.0 31.1 %copy-start.26 = (bf16[128,768]{1,0:T(8,128)(2,1)S(1)}, bf16[128,768]{1,0:T(8,128)(2,1)}, u32[]{:S(2)}) copy-start(bf16[128,768]{1,0:T(8,128)(2,1)} %param.38) | copy-start | bytes 589828
  146.9 0.6 copy-start.15
  149.8 2.7 %copy-start.25 = (bf16[172,768]{1,0:T(8,128)(2,1)S(1)}, bf16[172,768]{1,0:T(8,128)(2,1)}, u32[]{:S(2)}) copy-start(bf16[172,768]{1,0:T(8,128)(2,1)} %param.39) | copy-start | bytes 792580
  149.8 2.7 %copy-start.27 = (bf16[1,256,172]{1,2,0:T(8,128)(2,1)S(1)}, bf16[1,256,172]{1,2,0:T(8,128)(2,1)}, u32[]{:S(2)}) copy-start(bf16[1,256,172]{1,2,0:T(8,128)(2,1)} %param.32) | copy-start | bytes 264196
  149.8 2.7 %copy-start.32 = (f32[768]{0:T(1024)S(1)}, f32[768]{0:T(1024)}, u32[]{:S(2)}) copy-start(f32[768]{0:T(1024)} %param.40) | copy-start | bytes 9220
  151.1 2.7 %copy-start.35 = (f32[128]{0:T(128)S(1)}, f32[128]{0:T(128)}, u32[]{:S(2)}) copy-start(f32[128]{0:T(128)} %param.36) | copy-start | bytes 1540
  151.1 2.7 %copy-start.36 = (f32[128]{0:T(128)S(1)}, f32[128]{0:T(128)}, u32[]{:S(2)}) copy-start(f32[128]{0:T(128)} %param.35) | copy-start | bytes 1540
  152.5 18.1 %copy-start.3 = (bf16[64,8,16,128]{3,2,1,0:T(8,128)(2,1)S(1)}, bf16[64,8,16,128]{3,2,1,0:T(8,128)(2,1)}, u32[]{:S(2)}) copy-start(bf16[64,8,16,128]{3,2,1,0:T(8,128)(2,1)} %all_to_all.25) | copy-start | bytes 6291460
  180.5 1.4 copy-start.2
  181.9 5.7 %copy-start.10 = (bf16[512,128]{1,0:T(8,128)(2,1)}, bf16[512,128]{1,0:T(8,128)(2,1)S(1)}, u32[]{:S(2)}) copy-start(bf16[512,128]{1,0:T(8,128)(2,1)S(1)} %slice.22.left_ref) | copy-start | bytes 393220
  181.9 1.2 copy-start.6
  183.1 1.0 copy-start.8
  184.1 0.9 copy-start.12
  187.6 0.7 copy-start.20
  188.2 4.9 %copy-start.30 = (s32[1,256]{1,0:T(1,128)S(1)}, s32[1,256]{1,0:T(1,128)}, u32[]{:S(2)}) copy-start(s32[1,256]{1,0:T(1,128)} %param.26) | copy-start | bytes 3076
  189.3 32.8 %all-to-all-start.3 = ((bf16[8,256,256]{2,1,0:T(8,128)(2,1)}), bf16[8,256,256]{2,1,0:T(8,128)(2,1)S(1)}, u32[]{:S(2)}, u32[]{:S(2)}) async-start(bf16[8,256,256]{2,1,0:T(8,128)(2,1)} %broadcast_in_dim.42), calls=%async_computation.3 | async-start | bytes 2097152 | tf_op jit(solution)/shard_map/all_to_all | solution.py:396
  197.7 1.8 copy-start.14
  197.7 1.8 copy-start.16
  199.5 22.5 %copy-start.34 = (s32[256]{0:T(256)S(1)}, s32[256]{0:T(256)}, u32[]{:S(2)}) copy-start(s32[256]{0:T(256)} %select_reduce_fusion.1) | copy-start | bytes 3076
  199.5 22.6 %copy-start.22 = (f32[256]{0:T(256)S(1)}, f32[256]{0:T(256)}, u32[]{:S(2)}) copy-start(f32[256]{0:T(256)} %param.46) | copy-start | bytes 3076
  199.5 22.6 %copy-start.23 = (f32[256]{0:T(256)S(1)}, f32[256]{0:T(256)}, u32[]{:S(2)}) copy-start(f32[256]{0:T(256)} %param.48) | copy-start | bytes 3076
  222.1 3.4 %copy-start.1 = (bf16[8192,512]{1,0:T(8,128)(2,1)S(1)}, bf16[8192,512]{1,0:T(8,128)(2,1)}, u32[]{:S(2)}) copy-start(bf16[8192,512]{1,0:T(8,128)(2,1)} %shard_map.251.keyval_ref) | copy-start | bytes 25165828
  225.5 0.9 copy-start.5
  226.4 0.9 copy-start.11
  227.3 0.9 copy-start.17
  228.3 0.9 copy-start.18
  229.2 0.9 copy-start.19
  230.1 0.9 copy-start.21
  231.0 16.9 %copy-start.31 = (s32[2048]{0:T(1024)S(1)}, s32[2048]{0:T(1024)}, u32[]{:S(2)}) copy-start(s32[2048]{0:T(1024)} %select_reduce_fusion) | copy-start | bytes 24580
  231.0 17.2 %copy-start.9 = (bf16[2048,256]{1,0:T(8,128)(2,1)S(1)}, bf16[2048,256]{1,0:T(8,128)(2,1)}, u32[]{:S(2)}) copy-start(bf16[2048,256]{1,0:T(8,128)(2,1)} %start_ref.1) | copy-start | bytes 3145732
Sparse Core Ops, SparseCore 0:
  10.7 54.3 all-gather.3

commit v2 on v1

v2 whole, which is shorter than its diff:
```python
import jax
import jax.numpy as jnp
from jax import lax
from jax.experimental import pallas as pl
from jax.experimental.pallas import tpu as pltpu
from jax.sharding import Mesh, PartitionSpec as P

HEADS = 2
TILE = 128
PLANE = ("x", "c", "y", "zp")
VMEM = pl.BlockSpec(memory_space=pltpu.VMEM)
SMEM = pl.BlockSpec(memory_space=pltpu.SMEM)
ANY = pl.BlockSpec(memory_space=pl.ANY)
F32 = jnp.float32
BF16 = jnp.bfloat16


def params(mib):
    return pltpu.CompilerParams(vmem_limit_bytes=mib * 2**20)


def dot(a, b):
    return jnp.dot(a, b, preferred_element_type=F32)


def time_code(delta, time_freq, time_phase):
    angle = delta.astype(F32)[..., None] * time_freq + time_phase
    return jnp.cos(angle).astype(BF16)


def copies_of(pairs, sems):
    return [
        pltpu.make_async_copy(source, target, sems.at[place])
        for place, (source, target) in enumerate(pairs)
    ]


def start_copies(pairs, sems):
    copies = copies_of(pairs, sems)
    for copy in copies:
        copy.start()
    return copies


def select_kernel(req_ref, ring_any, out_ref, ring, sems):
    dests, blocks = out_ref.shape[:2]
    copies = start_copies(
        [(ring_any.at[block], ring.at[block]) for block in range(blocks)], sems
    )
    group = 8
    for block in range(blocks):
        copies[block].wait()

        def body(step, carry):
            for place in range(group):
                dest = step * group + place
                out_ref[dest, block] = ring[block, req_ref[dest * blocks + block]]
            return carry

        lax.fori_loop(0, dests // group, body, 0)


def select_tiles(requests, ring):
    blocks, _, rows, width = ring.shape
    dests = requests.shape[0]
    return pl.pallas_call(
        select_kernel,
        out_shape=jax.ShapeDtypeStruct((dests, blocks, rows, width), ring.dtype),
        in_specs=[SMEM, ANY],
        out_specs=VMEM,
        scratch_shapes=[pltpu.VMEM(ring.shape, ring.dtype), pltpu.SemaphoreType.DMA((blocks,))],
        compiler_params=params(16),
        cost_estimate=pl.CostEstimate(flops=0, bytes_accessed=6 * 2**20, transcendentals=0),
    )(requests.reshape(-1), ring)


def table_copies(table_any, table, sems, chunk):
    pairs = []
    for first in range(0, table.shape[0], chunk):
        at = pl.ds(first, chunk)
        pairs.append((table_any.at[at, :], table.at[at, :]))
    return start_copies(pairs, sems)


def widen(copies, table, lows, highs, chunk):
    half = lows.shape[1]
    step_rows = 128
    for place, copy in enumerate(copies):
        copy.wait()

        def body(step, carry):
            first = pl.multiple_of(place * chunk + step * step_rows, step_rows)
            at = pl.ds(first, step_rows)
            lows[at, :] = table[at, :half].astype(F32)
            highs[at, :] = table[at, half:].astype(F32)
            return carry

        lax.fori_loop(0, chunk // step_rows, body, 0)


def gather_block(index_ref, first, lows, highs, low_out, high_out):
    for lane in range(low_out.shape[0]):
        row = index_ref[first + lane]
        low_out[pl.ds(lane, 1), :] = lows[pl.ds(row, 1), :]
        high_out[pl.ds(lane, 1), :] = highs[pl.ds(row, 1), :]


CHUNKS = 8


def update_kernel(
    index_ref,
    table_any,
    base_any,
    hid_any,
    same_any,
    source_any,
    weight_any,
    written_ref,
    pair_ref,
    table,
    lows,
    highs,
    low_pick,
    high_pick,
    base,
    hid,
    same,
    source,
    weight,
    sems,
    table_sems,
):
    pairs, width = pair_ref.shape
    events = pairs // 2
    chunk = table.shape[0] // CHUNKS
    arrivals = table_copies(table_any, table, table_sems, chunk)
    copies = start_copies(
        [
            (base_any, base),
            (hid_any, hid),
            (same_any, same),
            (source_any, source),
            (weight_any, weight),
        ],
        sems,
    )
    widen(arrivals, table, lows, highs, chunk)
    block = low_pick.shape[0]

    def body(step, carry):
        first = pl.multiple_of(step * block, block)
        gather_block(index_ref, first, lows, highs, low_pick, high_pick)
        picked = jnp.concatenate([low_pick[...], high_pick[...]], axis=1)
        pair_ref[pl.ds(first, block), :] = picked.astype(BF16)
        return carry

    lax.fori_loop(0, pairs // block, body, 0)
    for copy in copies:
        copy.wait()
    pre = base[...] + dot(pair_ref[:events, :], weight[...])
    tally = jnp.sum(same[...], axis=1, keepdims=True)
    summed = jnp.dot(
        same[...], pre, preferred_element_type=F32, precision=lax.Precision.HIGHEST
    )
    gate_in = summed / tally
    reset = jax.nn.sigmoid(gate_in[:, :width] + hid[:, :width])
    keep = jax.nn.sigmoid(gate_in[:, width : 2 * width] + hid[:, width : 2 * width])
    cand = jnp.tanh(gate_in[:, 2 * width :] + reset * hid[:, 2 * width :])
    state = source[...].astype(F32)
    written_ref[...] = ((1.0 - keep) * cand + keep * state).astype(BF16)


def update_rows(index, table, base, hid, same, source, weight):
    events, width = source.shape
    rows = table.shape[0]
    half, block = width // 2, 64
    held = [base, hid, same, source, weight]
    return pl.pallas_call(
        update_kernel,
        out_shape=(
            jax.ShapeDtypeStruct((events, width), BF16),
            jax.ShapeDtypeStruct((2 * events, width), BF16),
        ),
        in_specs=[SMEM] + [ANY] * 6,
        out_specs=(VMEM, VMEM),
        scratch_shapes=[
            pltpu.VMEM((rows, width), BF16),
            pltpu.VMEM((rows, half), F32),
            pltpu.VMEM((rows, half), F32),
            pltpu.VMEM((block, half), F32),
            pltpu.VMEM((block, half), F32),
        ]
        + [pltpu.VMEM(array.shape, array.dtype) for array in held]
        + [pltpu.SemaphoreType.DMA((len(held),)), pltpu.SemaphoreType.DMA((CHUNKS,))],
        compiler_params=params(24),
        cost_estimate=pl.CostEstimate(flops=10**9, bytes_accessed=8 * 2**20, transcendentals=0),
    )(index, table, *held)


def keyval_kernel(
    index_ref,
    table_any,
    code_any,
    weight_any,
    out_any,
    table,
    lows,
    highs,
    even_low,
    even_high,
    odd_low,
    odd_high,
    code,
    weight,
    out,
    sems,
    table_sems,
    out_sems,
):
    count = out.shape[0]
    block = even_low.shape[0]
    pairs = count // (2 * block)
    chunk = table.shape[0] // CHUNKS
    arrivals = table_copies(table_any, table, table_sems, chunk)
    copies = start_copies([(code_any, code), (weight_any, weight)], sems)
    widen(arrivals, table, lows, highs, chunk)

    def project(first, low, high):
        at = pl.ds(first, block)
        joined = [low[...].astype(BF16), high[...].astype(BF16), code[at, :]]
        out[at, :] = dot(jnp.concatenate(joined, axis=1), weight[...]).astype(BF16)

    def saved(step):
        at = pl.ds(pl.multiple_of(step * 2 * block, 2 * block), 2 * block)
        return pltpu.make_async_copy(out.at[at, :], out_any.at[at, :], out_sems.at[step])

    gather_block(index_ref, 0, lows, highs, even_low, even_high)
    for copy in copies:
        copy.wait()

    def body(step, carry):
        first = pl.multiple_of(step * 2 * block, 2 * block)
        second = pl.multiple_of(first + block, block)
        gather_block(index_ref, second, lows, highs, odd_low, odd_high)
        project(first, even_low, even_high)
        third = pl.multiple_of(jnp.where(step + 1 < pairs, first + 2 * block, 0), block)
        gather_block(index_ref, third, lows, highs, even_low, even_high)
        project(second, odd_low, odd_high)
        saved(step).start()
        return carry

    lax.fori_loop(0, pairs, body, 0)

    def finish(step, carry):
        saved(step).wait()
        return carry

    lax.fori_loop(0, pairs, finish, 0)


def keyval_rows(index, table, code, weight):
    count = index.shape[0]
    rows, width = table.shape
    half, block = width // 2, 512
    out = jax.ShapeDtypeStruct((count, weight.shape[1]), BF16)
    return pl.pallas_call(
        keyval_kernel,
        out_shape=out,
        in_specs=[SMEM] + [ANY] * 3,
        out_specs=ANY,
        scratch_shapes=[
            pltpu.VMEM((rows, width), BF16),
            pltpu.VMEM((rows, half), F32),
            pltpu.VMEM((rows, half), F32),
            pltpu.VMEM((block, half), F32),
            pltpu.VMEM((block, half), F32),
            pltpu.VMEM((block, half), F32),
            pltpu.VMEM((block, half), F32),
            pltpu.VMEM(code.shape, BF16),
            pltpu.VMEM(weight.shape, BF16),
            pltpu.VMEM(out.shape, BF16),
            pltpu.SemaphoreType.DMA((2,)),
            pltpu.SemaphoreType.DMA((CHUNKS,)),
            pltpu.SemaphoreType.DMA((count // (2 * block),)),
        ],
        compiler_params=params(32),
        cost_estimate=pl.CostEstimate(
            flops=2 * count * weight.shape[0] * weight.shape[1],
            bytes_accessed=16 * 2**20,
            transcendentals=0,
        ),
    )(index, table, code, weight)


def one_hot(row, total):
    behind = row - lax.broadcasted_iota(jnp.int32, row.shape, 1)
    return jnp.concatenate(
        [jnp.where(behind == first, 1.0, 0.0).astype(BF16) for first in range(0, total, TILE)],
        axis=1,
    )


def newest(row, rows, held):
    known = jnp.concatenate([row] * (rows.shape[1] // TILE), axis=1) >= 0
    return jnp.where(known, dot(one_hot(row, rows.shape[0]), rows), held.astype(F32)).astype(BF16)


def final_kernel(
    rows_any,
    before_any,
    source_any,
    weight_any,
    after_any,
    start_any,
    keyval_any,
    pair_any,
    small_any,
    logits_ref,
    memory_any,
    rows,
    before,
    source,
    weight,
    after,
    start,
    keyval_ref,
    pair,
    small,
    memory,
    queries,
    attended,
    sems,
):
    events, width = source.shape
    head = width // HEADS
    neighbours = keyval_ref.shape[0] // events
    copies = start_copies(
        [
            (before_any, before),
            (rows_any, rows),
            (source_any, source),
            (weight_any, weight),
            (after_any, after),
            (start_any, start),
            (keyval_any, keyval_ref),
            (pair_any, pair),
            (small_any, small),
        ],
        sems,
    )
    for copy in copies[:3]:
        copy.wait()
    current = newest(before[...], rows[...], source[...])
    copies[3].wait()
    queries[...] = dot(current, weight[:width, :]).astype(BF16).astype(F32)
    copies[4].wait()
    copies[5].wait()
    block = 1024

    def update(step, carry):
        at = pl.ds(pl.multiple_of(step * block, block), block)
        memory[at, :] = newest(after[at, :], rows[...], start[at, :])
        return carry

    lax.fori_loop(0, memory.shape[0] // block, update, 0)
    saved = pltpu.make_async_copy(memory, memory_any, sems.at[9])
    saved.start()
    for copy in copies[6:]:
        copy.wait()

    group, batch = 8, 8
    columns = group * neighbours
    owner = lax.broadcasted_iota(jnp.int32, (HEADS * group, columns), 1) // neighbours
    event = lax.broadcasted_iota(jnp.int32, (HEADS * group, columns), 0) % group
    own = owner == event
    low = lax.broadcasted_iota(jnp.int32, (group, width), 1) < head
    scale = 1.0 / jnp.sqrt(F32(head))

    def body(step, carry):
        firsts = [step * batch + place for place in range(batch)]
        ats = [pl.ds(pl.multiple_of(first * columns, columns), columns) for first in firsts]
        lines = [pl.ds(pl.multiple_of(first * group, group), group) for first in firsts]
        scores = []
        for at, line in zip(ats, lines):
            query = queries[line, :]
            zero = jnp.zeros_like(query)
            stacked = jnp.concatenate(
                [jnp.where(low, query, zero), jnp.where(low, zero, query)], axis=0
            ).astype(BF16)
            scores.append(
                lax.dot_general(
                    stacked,
                    keyval_ref[at, :width],
                    (((1,), (1,)), ((), ())),
                    preferred_element_type=F32,
                )
            )
        scores = [jnp.where(own, score * scale, -jnp.inf) for score in scores]
        tops = [jnp.max(score, axis=1, keepdims=True) for score in scores]
        powers = [jnp.exp(score - top) for score, top in zip(scores, tops)]
        totals = [jnp.sum(power, axis=1, keepdims=True) for power in powers]
        shares = [(power / total).astype(BF16) for power, total in zip(powers, totals)]
        mixes = [dot(part, keyval_ref[at, width:]) for part, at in zip(shares, ats)]
        for mixed, line in zip(mixes, lines):
            attended[line, :] = jnp.where(low, mixed[:group, :], mixed[group:, :])
        return carry

    lax.fori_loop(0, events // group // batch, body, 0)
    embedding = dot(attended[...].astype(BF16), weight[width : 2 * width, :])
    embedding = embedding + dot(current, weight[2 * width : 3 * width, :]) + small[0:1, :]
    embedding = jnp.maximum(embedding, 0.0).astype(BF16)
    embed_part = dot(embedding, weight[3 * width : 4 * width, :])
    other_part = dot(pair[...], weight[4 * width :, :])
    for side in range(2):
        hidden = embed_part + other_part[side * events : (side + 1) * events, :]
        hidden = jnp.maximum(hidden + small[1:2, :], 0.0).astype(BF16)
        logits_ref[side : side + 1, :] = lax.dot_general(
            small[2:3, :].astype(BF16),
            hidden,
            (((1,), (1,)), ((), ())),
            preferred_element_type=F32,
        )
    saved.wait()


def final_step(*held):
    rows, before, source, weight, after, start, keyval, pair, small = held
    events, width = source.shape
    return pl.pallas_call(
        final_kernel,
        out_shape=(
            jax.ShapeDtypeStruct((2, events), F32),
            jax.ShapeDtypeStruct(start.shape, BF16),
        ),
        in_specs=[ANY] * len(held),
        out_specs=(VMEM, ANY),
        scratch_shapes=[pltpu.VMEM(array.shape, array.dtype) for array in held]
        + [
            pltpu.VMEM(start.shape, BF16),
            pltpu.VMEM((events, width), F32),
            pltpu.VMEM((events, width), F32),
            pltpu.SemaphoreType.DMA((len(held) + 1,)),
        ],
        compiler_params=params(28),
        cost_estimate=pl.CostEstimate(
            flops=4 * 10**9, bytes_accessed=12 * 2**20, transcendentals=0
        ),
    )(*held)


def shards(
    memory_start,
    src_row,
    dst_pos,
    neg_pos,
    nbr_pos,
    event_time,
    nbr_time,
    edge_feat,
    tile_req,
    tile_count,
    time_freq,
    time_phase,
    msg_memory,
    msg_time,
    msg_edge,
    bias_input,
    hid_weight,
    bias_hidden,
    query_weight,
    keyval_weight,
    out_weight,
    bias_out,
    pred_weight,
    bias_pred,
    logit_weight,
):
    nx, nc, ny, nzq, nzp = (lax.axis_size(name) for name in ("x", "c", "y", "zq", "zp"))
    batches = nx * nc
    owners = ny * nzq * nzp
    node_rows, width = memory_start.shape
    events = src_row.shape[1]
    neighbours = nbr_pos.shape[2]
    tiles = node_rows // TILE
    share = TILE // batches
    batch = lax.axis_index("x") * nc + lax.axis_index("c")

    own_share = lax.dynamic_index_in_dim(
        memory_start.reshape(tiles, batches, share, width), batch, 1, False
    )
    sources = src_row.reshape(events)
    wanted = tile_req.reshape(ny, nzq, nzp).transpose(0, 2, 1).reshape(1, ny * nzp, nzq)
    wanted = jnp.broadcast_to(wanted, (batches, ny * nzp, nzq)).reshape(-1, nzq)
    told = jnp.broadcast_to(sources[None], (wanted.shape[0], events))
    heard = lax.all_to_all(
        jnp.concatenate([wanted, told], axis=1), PLANE, 0, 0, tiled=True
    )
    asked = heard[:, :nzq]
    heard = heard[:, nzq:].reshape(batches, ny, nzp, events)
    heard = lax.dynamic_index_in_dim(heard, lax.axis_index("y"), 1, False)
    all_sources = lax.dynamic_index_in_dim(heard, lax.axis_index("zp"), 1, False).reshape(-1)

    running = jnp.cumsum(tile_count.reshape(owners))

    def table_rows(position):
        owner = jnp.sum((running <= (position // TILE)[..., None]).astype(jnp.int32), axis=-1)
        row = position % TILE
        oy, ozq, ozp = owner // (nzq * nzp), (owner // nzp) % nzq, owner % nzp
        source = ((row // share) * ny + oy) * nzp + ozp
        return (source * nzq + ozq) * share + row % share

    dst_rows = table_rows(dst_pos.reshape(events))
    neg_rows = table_rows(neg_pos.reshape(events))
    nbr_rows = table_rows(nbr_pos.reshape(events * neighbours))
    pair_rows = jnp.concatenate([dst_rows, neg_rows])

    event_times = event_time.reshape(events)
    past_times = nbr_time.reshape(events, neighbours)
    ages = event_times[:, None] - past_times
    code = time_code(ages.reshape(-1), time_freq, time_phase)
    source_mem = memory_start[sources]
    base = dot(source_mem, msg_memory[:width])
    base = base + dot(time_code(ages[:, 0], time_freq, time_phase), msg_time)
    base = base + dot(edge_feat.reshape(events, -1), msg_edge)
    base = base + bias_input
    hid = dot(source_mem, hid_weight) + bias_hidden
    same = (sources[:, None] == sources[None, :]).astype(F32)
    order = jnp.arange(batches * events, dtype=jnp.int32)
    of_batch = order // events
    node_ids = jnp.arange(node_rows, dtype=jnp.int32)
    upto = jnp.where(of_batch <= batch, all_sources, -1)
    earlier = jnp.where(of_batch < batch, all_sources, -1)
    after_row = jnp.max(jnp.where(upto[None, :] == node_ids[:, None], order[None, :], -1), axis=1)
    before_row = jnp.max(jnp.where(earlier[None, :] == sources[:, None], order[None, :], -1), axis=1)
    after_row = jnp.broadcast_to(after_row[:, None], (node_rows, TILE))
    before_row = jnp.broadcast_to(before_row[:, None], (events, TILE))

    weights = jnp.concatenate([query_weight, out_weight, pred_weight])
    small = jnp.stack([bias_out, bias_pred, logit_weight.astype(F32)])
    small = jnp.concatenate([small, jnp.zeros((5, width), F32)])
    target_weight = msg_memory[width:]

    ring = lax.all_gather(own_share, "zq")
    table = lax.all_to_all(select_tiles(asked, ring), PLANE, 0, 0, tiled=True)
    table = table.reshape(-1, width)
    base, after_row, before_row = lax.optimization_barrier((base, after_row, before_row))
    written, pair = update_rows(pair_rows, table, base, hid, same, source_mem, target_weight)
    rows = lax.all_to_all(
        jnp.broadcast_to(written[None], (batches, events, width)), ("x", "c"), 0, 0, tiled=True
    ).reshape(-1, width)
    keyval = keyval_rows(nbr_rows, table, code, keyval_weight)
    logits, memory_after = final_step(
        rows,
        before_row,
        source_mem,
        weights,
        after_row,
        memory_start,
        keyval,
        pair,
        small,
    )
    return (logits.reshape(2, 1, events), memory_after.reshape(1, node_rows, width))


def solution(mesh):
    grid = Mesh(mesh.devices.reshape(4, 2, 4, 8, 2), ("x", "c", "y", "zq", "zp"))
    tm, dom = ("x", "c"), ("y", "zq", "zp")
    by_event = [P(tm, dom), P(tm, dom, None)]
    in_specs = (
        P(dom, None),
        by_event[0],
        by_event[0],
        by_event[0],
        by_event[1],
        by_event[0],
        by_event[1],
        by_event[1],
        by_event[1],
        by_event[1],
    ) + (P(),) * 15
    out_specs = (P(None, tm, dom), P(tm, dom, None))
    return jax.shard_map(
        shards, mesh=grid, in_specs=in_specs, out_specs=out_specs, check_vma=False
    )
```

time: 262 us -> 198 us (0.76)
  blocking collectives: 79.4 us -> 18.5 us
  Pallas kernels: 57.7 us -> 33.5 us
  waiting for transfers between devices: 35.4 us -> 58.5 us
  other arithmetic: 31.5 us -> 23.9 us
  starting transfers between devices: 8.3 us -> 15.2 us
    all_to_all x2 -> x1, blocking collectives: 58.7 us -> 18.5 us  [shards(): lax.all_to_all(jnp.concatenate([wanted, told], axis=1), PLANE, 0, 0, tile...]
    pallas_call x5 -> x3, Pallas kernels: 55.2 us -> 28.8 us  [the longest x1 17.9 us: keyval_rows(): pl.pallas_call(keyval_kernel, out_shape=out, in_specs=[SMEM] + [ANY] * 3,...]
    all_to_all x1, waiting for transfers between devices: 0.01 us -> 22.5 us  [shards(): table = lax.all_to_all(select_tiles(asked, ring), PLANE, 0, 0, tiled=True)]
    all_gather x1 -> x0, blocking collectives: 20.7 us -> none  [shards(): all_sources = lax.all_gather(sources, ('x', 'c')).reshape(-1)]
    all_to_all x1, starting transfers between devices: 4.4 us -> 10.7 us  [shards(): table = lax.all_to_all(select_tiles(asked, ring), PLANE, 0, 0, tiled=True)]
    unnamed x80 -> x63, local copies, waits for them, and re-layouts: 18 us -> 19.4 us
  transfers between devices with their start and end apart: 3 -> 3, of which waited for: 1 -> 2; matrix products, arithmetic and copies ran while one was open for 17% -> 18% of each run, Pallas kernels for 12% -> 9%
where the time goes in v2:
time: 198 us; the launch traced here: 197 us
  waiting for transfers between devices  58.5 us (30%)
  Pallas kernels  33.5 us (17%)
  local copies, waits for them, and re-layouts  28.7 us (14%)
  other arithmetic  23.9 us (12%)
  blocking collectives  18.5 us (9%)
  starting transfers between devices  15.2 us (8%)
  between operations  14.6 us (7%)
  matrix products  4.25 us (2%)
    all_gather x1, waiting for transfers between devices, shards(): ring = lax.all_gather(own_share, 'zq')  36 us
    all_to_all x1, waiting for transfers between devices, shards(): table = lax.all_to_all(select_tiles(asked, ring), PLANE, 0, 0, tiled=True)  22.5 us
    unnamed x63, local copies, waits for them, and re-layouts  19.4 us
    all_to_all x1, blocking collectives, shards(): lax.all_to_all(jnp.concatenate([wanted, told], axis=1), PLANE, 0, 0, tile...  18.5 us
    pallas_call x1, Pallas kernels, keyval_rows(): pl.pallas_call(keyval_kernel, out_shape=out, in_specs=[SMEM] + [ANY] * 3,...  17.9 us
    convert_element_type x1, other arithmetic, time_code(): return jnp.cos(angle).astype(BF16)  14.9 us
    all_to_all x1, starting transfers between devices, shards(): table = lax.all_to_all(select_tiles(asked, ring), PLANE, 0, 0, tiled=True)  10.7 us
    pallas_call x1, Pallas kernels, final_step(): pl.pallas_call(final_kernel, out_shape=(jax.ShapeDtypeStruct((2, events),...  7.97 us
  transfers between devices with their start and end apart: 3, of which 2 were waited for; matrix products, arithmetic and copies ran while one was open for 18% of the time, Pallas kernels for 9%

profile of v2, /device:TPU:1, one launch (start us, length us, event | category | flops | bytes accessed | tf_op | source)
XLA Modules:
  0.0 197.1 jit_solution(11019833030221966821)
XLA Ops:
  7.2 0.0 copy-start
  7.2 0.0 all-gather.3.cloned.1.call-start
  7.2 1.6 constant_dynamic-slice_fusion.1
  8.8 0.0 all-gather.3.cloned.1.call-update
  8.9 0.8 pad.8.clone
  9.6 0.5 broadcast.339
  10.1 1.3 reduce.4
  11.5 0.1 reshape.253
  11.6 0.1 copy.45
  11.7 0.1 all_to_all.14
  11.8 18.5 %all_to_all.22 = s32[64,1,264]{2,1,0:T(1,128)S(1)} all-to-all(s32[64,1,264]{2,1,0:T(1,128)S(1)} %all_to_all.14), channel_id=1, replica_groups=mesh['x'=4,'c'=2,'y'=4,'zq'=8,'zp'=2] {'x','c','y','zp'}, dimensions={0} | all-to-all | bytes 135168 | tf_op jit(solution)/shard_map/all_to_all | solution.py:496
  30.3 0.1 reshape.255.req_ref
  30.4 36.0 %all-gather.3.cloned.1.call-done = bf16[128,1,16,256]{3,2,1,0:T(8,128)(2,1)} async-done(((bf16[16,1,16,256]{3,2,1,0:T(8,128)(2,1)}), bf16[128,1,16,256]{3,2,1,0:T(8,128)(2,1)}) %all-gather.3.cloned.1.call-update) | async-done | bytes 1048592 | tf_op jit(solution)/shard_map/all_gather | solution.py:544
  66.4 1.2 copy-done.8
  67.6 2.9 %shard_map.248 = bf16[64,8,16,256]{3,2,1,0:T(8,128)(2,1)S(1)} custom-call(s32[512]{0:T(512)S(1)} %reshape.255.req_ref, bf16[8,16,16,256]{3,2,1,0:T(8,128)(2,1)S(1)} %bitcast.36), custom_call_target="tpu_custom_call" | custom-call | bytes 6291456 | tf_op jit(solution)/shard_map/pallas_call | solution.py:66
  70.6 2.0 copy-done.1
  72.6 10.7 %all-to-all-start.1 = ((bf16[64,8,16,256]{3,2,1,0:T(8,128)(2,1)}), bf16[64,8,16,256]{3,2,1,0:T(8,128)(2,1)}, u32[]{:S(2)}, u32[]{:S(2)}) async-start(bf16[64,8,16,256]{3,2,1,0:T(8,128)(2,1)} %copy-done.1), calls=%async_computation.1 | async-start | bytes 8388608 | tf_op jit(solution)/shard_map/all_to_all | solution.py:545
  83.4 1.2 gather_fusion
  84.6 0.1 copy.44
  84.7 0.1 reduce-window.8
  84.7 0.1 reduce
  84.9 0.8 slice.19.weight_any
  85.7 0.1 copy.46
  85.8 0.1 reshape.264
  85.9 0.1 sub.88.clone
  86.0 0.1 sub.95
  86.1 0.1 copy.48
  86.2 0.1 reshape.265
  86.3 0.1 pad.3.clone
  86.4 0.1 convert_reduce_fusion.2
  86.6 0.1 maximum_maximum_fusion.small_any
  86.7 0.6 add_select_fusion.5
  87.3 0.8 compare_convert_fusion.same_any
  88.1 0.3 fusion.1
  88.4 0.3 convolution_add_fusion.hid_any
  88.7 1.6 convolution_add_fusion.2
  90.4 2.1 %fusion.base_any = f32[256,768]{1,0:T(8,128)} fusion(f32[256,768]{1,0:T(8,128)S(1)} %convolution_add_fusion.2, bf16[172,768]{1,0:T(8,128)(2,1)S(1)} %copy-done.16, f32[768]{0:T(1024)S(1)} %copy-done.21, bf16[1,256,172]{1,2,0:T(8,128)(2,1)} %param.32), kind=kOutput, calls=%fused_computation.8 | convolution fusion | flops 68026368 | bytes 1928192 | tf_op jit(solution)/shard_map/dot_general | solution.py:23
  92.4 14.9 %cosine_convert_fusion.code_any = bf16[8192,128]{1,0:T(8,128)(2,1)S(1)} fusion(f32[128]{0:T(128)} %param.36, f32[128]{0:T(128)} %param.35, f32[8192]{0:T(1024)S(1)} %subtract_convert_fusion), kind=kLoop, calls=%fused_computation.3 | loop fusion | flops 3145728 | bytes 2130944 | tf_op jit(solution)/shard_map/convert_element_type | solution.py:28
  107.4 0.7 slice.24
  108.1 0.9 reshape.261
  109.0 0.4 select_reduce_fusion.1
  109.4 2.3 %select_reduce_fusion = s32[2048]{0:T(1024)S(1)} fusion(s32[2048]{0:T(1024)S(1)} %get-tuple-element.27), kind=kLoop, calls=%fused_computation.1 | loop fusion | flops 12580864 | bytes 16384 | tf_op jit(solution)/shard_map/reduce_max | solution.py:534
  111.7 0.1 broadcast_in_dim.52.before_any
  111.8 1.4 broadcast_in_dim.49.after_any
  113.2 22.5 %all-to-all-done.1 = bf16[64,8,16,256]{3,2,1,0:T(8,128)(2,1)} async-done(((bf16[64,8,16,256]{3,2,1,0:T(8,128)(2,1)}), bf16[64,8,16,256]{3,2,1,0:T(8,128)(2,1)}, u32[]{:S(2)}, u32[]{:S(2)}) %all-to-all-start.1) | async-done | bytes 4194336 | tf_op jit(solution)/shard_map/all_to_all | solution.py:545
  135.7 1.1 copy-done.4
  136.8 1.0 copy-done.5
  137.8 0.9 copy-done.9
  138.7 4.7 %shard_map.249 = (bf16[256,256]{1,0:T(8,128)(2,1)S(1)}, bf16[512,256]{1,0:T(8,128)(2,1)S(1)}) custom-call(s32[512]{0:T(512)S(1)} %pad_add_fusion.1.index_ref, bf16[8192,256]{1,0:T(8,128)(2,1)} %bitcast.9.table_any, f32[256,768]{1,0:T(8,128)S(1)} %copy-done.4, f32[256,768]{1,0:T(8,128)S(1)} %convolution_add_fusion.hid_any, f32[256,256]{1,0:T(8,128)S(1)} %copy-done.9, ...), custom_call_target="tpu_custom_call" | custom-call | flops 1000000000 | bytes 8388608 | tf_op jit(solution)/shard_map/pallas_call | solution.py:179
  143.4 0.7 copy-done.12
  144.1 1.0 broadcast_in_dim.53
  145.2 4.5 %all-to-all-start.2 = ((bf16[8,256,256]{2,1,0:T(8,128)(2,1)}), bf16[8,256,256]{2,1,0:T(8,128)(2,1)}, u32[]{:S(2)}, u32[]{:S(2)}) async-start(bf16[8,256,256]{2,1,0:T(8,128)(2,1)} %broadcast_in_dim.53), calls=%async_computation.2 | async-start | bytes 2097152 | tf_op jit(solution)/shard_map/all_to_all | solution.py:549
  149.7 1.1 convert_reduce_fusion
  150.8 0.9 fusion.14.index_ref
  151.7 1.1 pad_maximum_fusion.weight_any
  152.8 1.0 copy-done.11
  153.8 17.9 %shard_map.250.keyval_any = bf16[8192,512]{1,0:T(8,128)(2,1)S(1)} custom-call(s32[8192]{0:T(1024)S(1)} %fusion.14.index_ref, bf16[8192,256]{1,0:T(8,128)(2,1)} %bitcast.9.table_any, bf16[8192,128]{1,0:T(8,128)(2,1)S(1)} %cosine_convert_fusion.code_any, bf16[384,512]{1,0:T(8,128)(2,1)S(1)} %copy-done.11), custom_call_target="tpu_custom_call" | custom-call | flops 3221225472 | bytes 16777216 | tf_op jit(solution)/shard_map/pallas_call | solution.py:267
  171.7 3.2 %copy-done.2 = bf16[8192,512]{1,0:T(8,128)(2,1)} copy-done((bf16[8192,512]{1,0:T(8,128)(2,1)}, bf16[8192,512]{1,0:T(8,128)(2,1)S(1)}, u32[]{:S(2)}) %copy-start.2) | copy-done | bytes 8388632
  175.0 3.4 %copy-done.3 = bf16[8192,512]{1,0:T(8,128)(2,1)S(1)} copy-done((bf16[8192,512]{1,0:T(8,128)(2,1)S(1)}, bf16[8192,512]{1,0:T(8,128)(2,1)}, u32[]{:S(2)}) %copy-start.3) | copy-done | bytes 8388632
  178.3 1.2 copy-done.7
  179.6 1.2 copy-done.10
  180.8 0.9 copy-done.13
  181.7 8.0 %shard_map.251 = (f32[2,256]{1,0:T(2,128)S(1)}, bf16[2048,256]{1,0:T(8,128)(2,1)}) custom-call(bf16[2048,256]{1,0:T(8,128)(2,1)} %bitcast.17.rows_any, s32[256,128]{1,0:T(8,128)S(1)} %broadcast_in_dim.52.before_any, bf16[256,256]{1,0:T(8,128)(2,1)S(1)} %gather_fusion, bf16[1280,256]{1,0:T(8,128)(2,1)S(1)} %pad_maximum_fusion.weight_any, ...), custom_call_target="tpu_custom_call" | custom-call | flops 4000000000 | bytes 12582912 | tf_op jit(solution)/shard_map/pallas_call | solution.py:430
  189.7 0.6 copy.49
  (62 shorter events, 0.3 us)
Async XLA Ops:
  7.2 81.2 %copy-start = (bf16[256,768]{1,0:T(8,128)(2,1)S(1)}, bf16[256,768]{1,0:T(8,128)(2,1)}, u32[]{:S(2)}) copy-start(bf16[256,768]{1,0:T(8,128)(2,1)} %param.41) | copy-start | bytes 1179652
  7.2 59.2 %all-gather.3.cloned.1.call-start = ((), (), s32[]{:S(2)}) async-start(), calls=%async_computation.3 | async-start | bytes 1179648 | tf_op jit(solution)/shard_map/all_gather | solution.py:544
  66.4 1.2 copy-start.8
  70.5 2.0 %copy-start.1 = (bf16[64,8,16,256]{3,2,1,0:T(8,128)(2,1)}, bf16[64,8,16,256]{3,2,1,0:T(8,128)(2,1)S(1)}, u32[]{:S(2)}) copy-start(bf16[64,8,16,256]{3,2,1,0:T(8,128)(2,1)S(1)} %shard_map.248) | copy-start | bytes 12582916
  72.5 10.8 %copy-start.19 = (s32[1,256]{1,0:T(1,128)S(1)}, s32[1,256]{1,0:T(1,128)}, u32[]{:S(2)}) copy-start(s32[1,256]{1,0:T(1,128)} %param.26) | copy-start | bytes 3076
  72.5 10.9 %copy-start.6 = (bf16[2048,256]{1,0:T(8,128)(2,1)S(1)}, bf16[2048,256]{1,0:T(8,128)(2,1)}, u32[]{:S(2)}) copy-start(bf16[2048,256]{1,0:T(8,128)(2,1)} %start_any.1) | copy-start | bytes 3145732
  72.5 12.0 %copy-start.27 = (s32[1,1,64]{2,1,0:T(1,128)S(1)}, s32[1,1,64]{2,1,0:T(1,128)}, u32[]{:S(2)}) copy-start(s32[1,1,64]{2,1,0:T(1,128)} %param.34) | copy-start | bytes 772
  72.5 12.3 %copy-start.14 = (bf16[512,768]{1,0:T(8,128)(2,1)S(1)}, bf16[512,768]{1,0:T(8,128)(2,1)}, u32[]{:S(2)}) copy-start(bf16[512,768]{1,0:T(8,128)(2,1)} %param.37) | copy-start | bytes 2359300
  72.5 13.1 %copy-start.18 = (s32[1,256,32]{1,2,0:T(8,128)S(1)}, s32[1,256,32]{1,2,0:T(8,128)}, u32[]{:S(2)}) copy-start(s32[1,256,32]{1,2,0:T(8,128)} %param.29) | copy-start | bytes 98308
  72.6 13.3 %copy-start.22 = (s32[1,256]{1,0:T(1,128)S(1)}, s32[1,256]{1,0:T(1,128)}, u32[]{:S(2)}) copy-start(s32[1,256]{1,0:T(1,128)} %param.30) | copy-start | bytes 3076
  72.6 13.5 %copy-start.17 = (s32[1,256,32]{1,2,0:T(8,128)S(1)}, s32[1,256,32]{1,2,0:T(8,128)}, u32[]{:S(2)}) copy-start(s32[1,256,32]{1,2,0:T(8,128)} %param.31) | copy-start | bytes 98308
  72.6 13.7 %copy-start.28 = (bf16[256]{0:T(256)(128)(2,1)S(1)}, bf16[256]{0:T(256)(128)(2,1)}, u32[]{:S(2)}) copy-start(bf16[256]{0:T(256)(128)(2,1)} %param.49) | copy-start | bytes 1540
  72.6 13.8 %copy-start.23 = (s32[1,256]{1,0:T(1,128)S(1)}, s32[1,256]{1,0:T(1,128)}, u32[]{:S(2)}) copy-start(s32[1,256]{1,0:T(1,128)} %param.27) | copy-start | bytes 3076
  72.6 13.8 %copy-start.24 = (s32[1,256]{1,0:T(1,128)S(1)}, s32[1,256]{1,0:T(1,128)}, u32[]{:S(2)}) copy-start(s32[1,256]{1,0:T(1,128)} %param.28) | copy-start | bytes 3076
  72.6 14.0 %copy-start.25 = (f32[256]{0:T(256)S(1)}, f32[256]{0:T(256)}, u32[]{:S(2)}) copy-start(f32[256]{0:T(256)} %param.48) | copy-start | bytes 3076
  72.6 14.0 %copy-start.26 = (f32[256]{0:T(256)S(1)}, f32[256]{0:T(256)}, u32[]{:S(2)}) copy-start(f32[256]{0:T(256)} %param.46) | copy-start | bytes 3076
  72.6 63.0 %all-to-all-start.1 = ((bf16[64,8,16,256]{3,2,1,0:T(8,128)(2,1)}), bf16[64,8,16,256]{3,2,1,0:T(8,128)(2,1)}, u32[]{:S(2)}, u32[]{:S(2)}) async-start(bf16[64,8,16,256]{3,2,1,0:T(8,128)(2,1)} %copy-done.1), calls=%async_computation.1 | async-start | bytes 8388608 | tf_op jit(solution)/shard_map/all_to_all | solution.py:545
  83.3 5.1 %copy-start.20 = (f32[768]{0:T(1024)S(1)}, f32[768]{0:T(1024)}, u32[]{:S(2)}) copy-start(f32[768]{0:T(1024)} %param.42) | copy-start | bytes 9220
  83.3 7.0 %copy-start.16 = (bf16[172,768]{1,0:T(8,128)(2,1)S(1)}, bf16[172,768]{1,0:T(8,128)(2,1)}, u32[]{:S(2)}) copy-start(bf16[172,768]{1,0:T(8,128)(2,1)} %param.39) | copy-start | bytes 792580
  83.3 7.0 %copy-start.21 = (f32[768]{0:T(1024)S(1)}, f32[768]{0:T(1024)}, u32[]{:S(2)}) copy-start(f32[768]{0:T(1024)} %param.40) | copy-start | bytes 9220
  85.9 1.5 copy-start.15
  135.6 1.1 copy-start.4
  136.8 1.0 copy-start.5
  137.8 0.9 copy-start.9
  143.4 0.7 copy-start.12
  145.2 29.8 %all-to-all-start.2 = ((bf16[8,256,256]{2,1,0:T(8,128)(2,1)}), bf16[8,256,256]{2,1,0:T(8,128)(2,1)}, u32[]{:S(2)}, u32[]{:S(2)}) async-start(bf16[8,256,256]{2,1,0:T(8,128)(2,1)} %broadcast_in_dim.53), calls=%async_computation.2 | async-start | bytes 2097152 | tf_op jit(solution)/shard_map/all_to_all | solution.py:549
  152.8 1.0 copy-start.11
  171.7 3.2 %copy-start.2 = (bf16[8192,512]{1,0:T(8,128)(2,1)}, bf16[8192,512]{1,0:T(8,128)(2,1)S(1)}, u32[]{:S(2)}) copy-start(bf16[8192,512]{1,0:T(8,128)(2,1)S(1)} %shard_map.250.keyval_any) | copy-start | bytes 25165828
  175.0 3.4 %copy-start.3 = (bf16[8192,512]{1,0:T(8,128)(2,1)S(1)}, bf16[8192,512]{1,0:T(8,128)(2,1)}, u32[]{:S(2)}) copy-start(bf16[8192,512]{1,0:T(8,128)(2,1)} %copy-done.2) | copy-start | bytes 25165828
  178.3 1.2 copy-start.7
  179.6 1.2 copy-start.10
  180.8 0.9 copy-start.13
Sparse Core Ops, SparseCore 0:
  10.7 55.6 all-gather.2
